TPU v7x, 32 devices: a whole 2x2x4 slice. The times are simulated.
32 devices in a mesh: inv: 2 (over y), tracer: 4 (over z), band: 4 (over x, core).
Axes of the slice: x: 2, y: 2, z: 4, core: 2. Of those that a mesh axis runs over, the one named last changes fastest.
Arguments:
- tracer_state: float32 [32, 32, 48, 512], P(('inv', 'tracer'), 'band'), parts along dimension 0, may hold values from -6 to 6
- control: float32 [32, 32, 512], P(('inv', 'tracer'), 'band'), parts along dimension 0, may hold values from -6 to 6
- prior_tiles: float32 [8, 8, 8], replicated, may hold values from -1 to 1
- tile_index: int32 [4, 4], replicated, may hold values from 0 to 7, as said below
- region_map: int32 [32, 512], P('band'), may hold values from 0 to 21
- region_sigma: float32 [16, 22], P('tracer'), may hold values from 0.3 to 3
- zonal_courant: float32 [64, 48, 512], P(('inv', 'band'), None, 'tracer'), parts along dimension 0, may hold values from -0.3 to 0.3
- meridional_courant: float32 [64, 48, 512], P(('inv', 'band'), None, 'tracer'), parts along dimension 0, may hold values from -0.3 to 0.3
- vertical_diffusion: float32 [64, 48, 512], P(('inv', 'band'), None, 'tracer'), parts along dimension 0, may hold values from 0.02 to 0.2
Outputs:
- final_state: float32 [32, 32, 48, 512], P(('inv', 'tracer'), 'band'), parts along dimension 0
- emission: float32 [32, 32, 512], P(('inv', 'tracer'), 'band'), parts along dimension 0
There are 2 independent parts, one for each index of `inv`. A program takes and returns all parts, laid end to end along the dimension named above; an argument that names none is the same for every part. Nothing has to cross between parts.
Inputs may be any that keep to these rules, and one draw needn't show every extreme that they name: `tile_index`: each entry names one of the 8 tiles; 0 and 7 both occur.
All inputs are finite; a program needn't handle non-finite values.
Results may differ from a plain program's by a relative error of at most 0.000071.
Values sent between devices are 32-bit elements; how exact they have to be, the bound alone decides.
A program may use at most 128 MiB of HBM per device.

v0:
```python
import jax
import jax.numpy as jnp
from jax import lax
from jax.sharding import PartitionSpec as P

STEPS = 2


exact_dot = lax.Precision.HIGHEST


def padded_2(block, sides, width):
    for axis, dim in sides:
        count = lax.axis_size(axis)
        forward = [(i, i + 1) for i in range(count - 1)]
        backward = [(target, source) for source, target in forward]
        low = lax.ppermute(
            lax.slice_in_dim(block, block.shape[dim] - width, None, axis=dim), axis, forward
        )
        high = lax.ppermute(lax.slice_in_dim(block, 0, width, axis=dim), axis, backward)
        block = jnp.concatenate([low, block, high], axis=dim)
    return block


def passed_along(value, axis, by):
    count = lax.axis_size(axis)
    pairs = [(i, i + by) for i in range(count) if 0 <= i + by < count]
    return lax.ppermute(value, axis, pairs)


def vertical_mixing(tracer_now, mixing):
    levels = tracer_now.shape[2]
    upper_level = jnp.concatenate(
        [tracer_now[:, :, 1:], jnp.zeros_like(tracer_now[:, :, :1])], axis=2
    )
    open_top = (lax.broadcasted_iota(jnp.int32, (levels, 1), 0) < levels - 1).astype(jnp.float32)
    flux_up = mixing * (tracer_now - upper_level) * open_top
    flux_down = jnp.concatenate([jnp.zeros_like(flux_up[:, :, :1]), flux_up[:, :, :-1]], axis=2)
    return flux_up - flux_down


def advance(tracer_now, weather, sideways, north_open, source):
    zonal, zonal_west, meridional, meridional_south, mixing = weather
    west_side, east_side = sideways(tracer_now)
    flux_east = jnp.maximum(zonal, 0.0) * tracer_now + jnp.minimum(zonal, 0.0) * east_side
    flux_west = jnp.maximum(zonal_west, 0.0) * west_side + jnp.minimum(zonal_west, 0.0) * tracer_now
    padded = padded_2(tracer_now, (("band", 1),), 1)
    north_side = padded[:, 2:]
    south_side = padded[:, :-2]
    flux_north = (
        jnp.maximum(meridional, 0.0) * tracer_now + jnp.minimum(meridional, 0.0) * north_side
    ) * north_open
    flux_south = (
        jnp.maximum(meridional_south, 0.0) * south_side
        + jnp.minimum(meridional_south, 0.0) * tracer_now
    )
    result = (
        tracer_now
        - (flux_east - flux_west)
        - (flux_north - flux_south)
        - vertical_mixing(tracer_now, mixing)
    )
    return result.at[:, :, 0, :].add(source)


def on_device(
    tracer_state,
    control,
    prior_tiles,
    tile_index,
    region_map,
    region_sigma,
    zonal_courant,
    meridional_courant,
    vertical_diffusion,
):
    band_count = lax.axis_size("band")
    band_index = lax.axis_index("band")
    tiles_count = prior_tiles.shape[0]
    lat_rows = control.shape[1]
    choose = (
        tile_index[:, :, None] == lax.broadcasted_iota(jnp.int32, (1, 1, tiles_count), 2)
    ).astype(jnp.float32)
    own_row = lax.dynamic_slice_in_dim(choose, band_index, 1, 0)[0]
    blocks = jnp.einsum("bt,tmn->bmn", own_row, prior_tiles, precision=exact_dot)
    row_block = jnp.transpose(blocks, (1, 0, 2)).reshape(lat_rows, band_count * lat_rows)
    prior_field = jnp.einsum(
        "jm,kmn->kjn",
        row_block,
        lax.all_gather(control, "band", axis=1, tiled=True),
        precision=exact_dot,
    )
    regions = region_sigma.shape[1]
    onehot = (region_map[:, :, None] == lax.broadcasted_iota(jnp.int32, (1, 1, regions), 2)).astype(
        jnp.float32
    )
    cell_sigma = jnp.einsum("kr,jnr->kjn", region_sigma, onehot, precision=exact_dot)
    emission = cell_sigma * prior_field
    latitude = band_index * lat_rows + lax.broadcasted_iota(jnp.int32, (lat_rows, 1, 1), 0)
    north_open = (latitude < band_count * lat_rows - 1).astype(jnp.float32)
    south_row = passed_along(meridional_courant[-1:], "band", 1)
    zonal, meridional, mixing, south_edge = (
        lax.all_gather(zonal_courant, "tracer", axis=2, tiled=True),
        lax.all_gather(meridional_courant, "tracer", axis=2, tiled=True),
        lax.all_gather(vertical_diffusion, "tracer", axis=2, tiled=True),
        lax.all_gather(south_row, "tracer", axis=2, tiled=True),
    )
    weather = (
        zonal,
        jnp.roll(zonal, 1, axis=2),
        meridional,
        jnp.concatenate([south_edge, meridional[:-1]], axis=0),
        mixing,
    )

    def sideways(tracer_now):
        return (jnp.roll(tracer_now, 1, axis=3), jnp.roll(tracer_now, -1, axis=3))

    tracer_field = tracer_state
    for substep in range(STEPS):
        tracer_field = advance(tracer_field, weather, sideways, north_open, emission)
    return (tracer_field, emission)


def solution(mesh):
    in_specs = (
        P(("inv", "tracer"), "band", None, None),
        P(("inv", "tracer"), "band", None),
        P(),
        P(),
        P("band", None),
        P("tracer", None),
        P(("inv", "band"), None, "tracer"),
        P(("inv", "band"), None, "tracer"),
        P(("inv", "band"), None, "tracer"),
    )
    out_specs = (P(("inv", "tracer"), "band", None, None), P(("inv", "tracer"), "band", None))
    return jax.shard_map(
        on_device, mesh=mesh, in_specs=in_specs, out_specs=out_specs, check_vma=False
    )
```

profile of v0, /device:TPU:0, one launch (start us, length us, event | category | flops | bytes accessed | tf_op | source)
XLA Modules:
  0.0 150.7 jit_solution(13097804177532343057)
XLA Ops:
  0.7 4.0 %copy.21 = f32[4,8,48,512]{3,0,1,2:T(4,128)S(1)} copy(f32[4,8,48,512]{3,2,1,0:T(8,128)} %param.13) | data formatting | bytes 6291456 | tf_op args[0]
  4.6 1.1 fusion.42
  5.7 1.3 collective-permute-start
  7.0 3.8 %collective-permute-start.2 = (f32[4,1,48,512]{3,0,1,2:T(4,128)}, f32[4,1,48,512]{3,0,1,2:T(4,128)}, u32[]{:S(2)}, u32[]{:S(2)}) collective-permute-start(f32[4,1,48,512]{3,0,1,2:T(4,128)} %get-tuple-element.39), channel_id=1, source_target_pairs={{0,1},{1,2},{2,3},{4,5},{5,6},{6,7},{8,9},{9,10},{10,11},{12,13},{... | collective-permute-start | bytes 1179656 | tf_op jit(solution)/shard_map/ppermute | solution.py:17
  10.8 3.7 %collective-permute-start.1 = (f32[1,48,128]{2,1,0:T(8,128)S(1)}, f32[1,48,128]{2,1,0:T(8,128)S(1)}, u32[]{:S(2)}, u32[]{:S(2)}) collective-permute-start(f32[1,48,128]{2,1,0:T(8,128)S(1)} %slice.144), channel_id=1, source_target_pairs={{0,1},{1,2},{2,3},{4,5},{5,6},{6,7},{8,9},{9,10},{10,11},{12,13},{... | collective-permute-start | bytes 73736 | tf_op jit(solution)/shard_map/ppermute | solution.py:28
  14.6 4.8 %fusion.41 = (f32[4,8,48,511]{3,0,1,2:T(4,128)}, f32[4,8,48,511]{3,0,1,2:T(4,128)}) fusion(f32[4,8,48,512]{3,0,1,2:T(4,128)S(1)} %copy.21), kind=kLoop, calls=%fused_computation.65 | loop fusion | bytes 12558336 | tf_op jit(solution)/shard_map/jit(_roll_static)/slice | solution.py:117
  19.4 1.7 %fusion.40 = (f32[4,8,48,1]{3,0,1,2:T(4,128)}, f32[4,8,48,1]{3,0,1,2:T(4,128)}) fusion(f32[4,8,48,512]{3,0,1,2:T(4,128)S(1)} %copy.21), kind=kLoop, calls=%fused_computation.64 | loop fusion | bytes 24576 | tf_op jit(solution)/shard_map/jit(_roll_static)/slice | solution.py:117
  21.1 20.0 %all_gather.15 = f32[8,48,512]{2,1,0:T(8,128)S(1)} all-gather(f32[8,48,128]{2,1,0:T(8,128)S(1)} %copy-done.18), channel_id=1, replica_groups=mesh['inv'=2,'tracer'=4,'band'=4] {'tracer'}, dimensions={2}, use_global_device_ids=true | all-gather | bytes 983040 | tf_op jit(solution)/shard_map/all_gather | solution.py:103
  41.2 1.4 broadcast_maximum_fusion.1
  42.5 19.1 %all_gather.16 = f32[8,48,512]{2,1,0:T(8,128)} all-gather(f32[8,48,128]{2,1,0:T(8,128)S(1)} %copy-done.17), channel_id=1, replica_groups=mesh['inv'=2,'tracer'=4,'band'=4] {'tracer'}, dimensions={2}, use_global_device_ids=true | all-gather | bytes 983040 | tf_op jit(solution)/shard_map/all_gather | solution.py:104
  61.7 17.4 %all_gather.18 = f32[8,48,512]{2,1,0:T(8,128)S(1)} all-gather(f32[8,48,128]{2,1,0:T(8,128)S(1)} %copy-done.19), channel_id=1, replica_groups=mesh['inv'=2,'tracer'=4,'band'=4] {'tracer'}, dimensions={2}, use_global_device_ids=true | all-gather | bytes 983040 | tf_op jit(solution)/shard_map/all_gather | solution.py:105
  79.1 1.3 copy.32
  80.5 2.5 %broadcast_maximum_fusion = (f32[8,48,512]{2,1,0:T(8,128)}, f32[8,48,512]{2,1,0:T(8,128)}) fusion(f32[8,48,512]{2,1,0:T(8,128)} %all_gather.16), kind=kLoop, calls=%fused_computation.45 | loop fusion | flops 393216 | bytes 2359296 | tf_op jit(solution)/shard_map/max | solution.py:51
  83.9 6.0 %all_gather.19 = f32[4,32,512]{2,1,0:T(8,128)S(1)} all-gather(f32[4,8,512]{2,1,0:T(8,128)S(1)} %copy-done.20), channel_id=1, replica_groups=mesh['inv'=2,'tracer'=4,'band'=4] {'band'}, dimensions={1}, use_global_device_ids=true | all-gather | bytes 327680 | tf_op jit(solution)/shard_map/all_gather | solution.py:90
  90.2 6.1 %multiply_multiply_fusion.1 = f32[4,8,48,512]{3,0,1,2:T(4,128)S(1)} fusion(f32[4,8,47,512]{3,0,1,2:T(4,128)S(1)} %slice-done, f32[48]{0:T(128)S(1)} %compare_convert_fusion, f32[8,48,512]{2,0,1:T(8,128)} %copy.32, f32[4,8,48,512]{3,2,1,0:T(8,128)} %param.13), kind=kLoop, calls=%fused_computation.33 | loop fusion | flops 2359296 | bytes 10158272 | tf_op jit(solution)/shard_map/mul | solution.py:37
  96.6 1.3 copy-done.4
  100.8 13.4 %all_gather.17 = f32[1,48,512]{2,1,0:T(8,128)S(1)} all-gather(f32[1,48,128]{2,1,0:T(8,128)S(1)} %collective-permute-done.1), channel_id=1, replica_groups=mesh['inv'=2,'tracer'=4,'band'=4] {'tracer'}, dimensions={2}, use_global_device_ids=true | all-gather | bytes 122880 | tf_op jit(solution)/shard_map/all_gather | solution.py:106
  115.5 10.2 %fusion.12 = f32[4,8,48,512]{3,0,1,2:T(4,128)S(1)} fusion(f32[4,8,48,512]{3,0,1,2:T(4,128)S(1)} %copy-done.3, f32[4,1,48,512]{3,0,1,2:T(4,128)} %collective-permute-done.2, f32[4,1,48,512]{3,0,1,2:T(4,128)} %collective-permute-done, f32[4,8,48,1]{3,0,1,2:T(4,128)S(1)} %copy-done.12, f32[4,8,48,511]{3,0,1,2:T(4,128)S(1)} %copy-done.7, ...), kind=kLoop, calls=%fused_computation.15 | loop fusion | flops 18087936 | bytes 25886752 | tf_op jit(solution)/shard_map/sub | solution.py:58
  127.7 1.5 %multiply_multiply_fusion = f32[4,8,48,512]{3,0,1,2:T(4,128)S(1)} fusion(f32[4,8,48,512]{3,0,1,2:T(4,128)S(1)} %get-tuple-element.48, f32[4,8,47,512]{3,0,1,2:T(4,128)S(1)} %slice.180, f32[48]{0:T(128)S(1)} %compare_convert_fusion, f32[8,48,512]{2,0,1:T(8,128)S(1)} %copy-done.10), kind=kLoop, calls=%fused_computation.32 | loop fusion | flops 2359296 | bytes 10158272 | tf_op jit(solution)/shard_map/mul | solution.py:37
  130.2 1.3 collective-permute-start.3
  131.5 3.3 %collective-permute-start.4 = (f32[4,1,48,512]{3,0,1,2:T(4,128)S(1)}, f32[4,1,48,512]{3,0,1,2:T(4,128)S(1)}, u32[]{:S(2)}, u32[]{:S(2)}) collective-permute-start(f32[4,1,48,512]{3,0,1,2:T(4,128)S(1)} %get-tuple-element.33), channel_id=1, source_target_pairs={{0,1},{1,2},{2,3},{4,5},{5,6},{6,7},{8,9},{9,10},{10,11},{12,13},{... | collective-permute-start | bytes 1179656 | tf_op jit(solution)/shard_map/ppermute | solution.py:17
  135.4 2.5 %fusion.38 = (f32[4,8,48,511]{3,0,1,2:T(4,128)S(1)}, f32[4,8,48,511]{3,0,1,2:T(4,128)S(1)}) fusion(f32[4,8,48,512]{3,0,1,2:T(4,128)S(1)} %get-tuple-element.48), kind=kLoop, calls=%fused_computation.62 | loop fusion | bytes 12558336 | tf_op jit(solution)/shard_map/jit(_roll_static)/slice | solution.py:117
  138.0 9.2 %fusion.4 = f32[4,8,48,512]{3,0,1,2:T(4,128)S(1)} fusion(f32[4,8,48,512]{3,0,1,2:T(4,128)S(1)} %get-tuple-element.48, f32[4,1,48,512]{3,0,1,2:T(4,128)S(1)} %collective-permute-done.4, f32[4,1,48,512]{3,0,1,2:T(4,128)S(1)} %collective-permute-done.3, f32[4,8,48,1]{3,0,1,2:T(4,128)S(1)} %get-tuple-element.29, f32[4,8,48,511]{3,0,1,2:T(4,128)S(1)} %get-tuple-element.31, ...), kind=kLoop, calls=%fused_computation.5 | loop fusion | flops 18087936 | bytes 25886752 | tf_op jit(solution)/shard_map/sub | solution.py:58
  147.2 3.5 %copy.37 = f32[4,8,48,512]{3,2,1,0:T(8,128)} copy(f32[4,8,48,512]{3,0,1,2:T(4,128)S(1)} %fusion.30) | data formatting | bytes 6291456
  (81 shorter events, 9.2 us)
Async XLA Ops:
  0.6 83.0 %copy-start = (f32[8,8,8]{2,1,0:T(8,128)S(1)}, f32[8,8,8]{2,1,0:T(8,128)}, u32[]{:S(2)}) copy-start(f32[8,8,8]{2,1,0:T(8,128)} %param.15) | copy-start | bytes 6148
  0.6 10.2 %copy-start.17 = (f32[8,48,128]{2,1,0:T(8,128)S(1)}, f32[8,48,128]{2,1,0:T(8,128)}, u32[]{:S(2)}) copy-start(f32[8,48,128]{2,1,0:T(8,128)} %param.20) | copy-start | bytes 589828
  4.6 14.8 %copy-start.2 = (f32[4,8,48,512]{3,0,1,2:T(4,128)}, f32[4,8,48,512]{3,0,1,2:T(4,128)S(1)}, u32[]{:S(2)}) copy-start(f32[4,8,48,512]{3,0,1,2:T(4,128)S(1)} %copy.21) | copy-start | bytes 9437188
  5.7 109.6 %collective-permute-start = (f32[4,1,48,512]{3,0,1,2:T(4,128)}, f32[4,1,48,512]{3,0,1,2:T(4,128)}, u32[]{:S(2)}, u32[]{:S(2)}) collective-permute-start(f32[4,1,48,512]{3,0,1,2:T(4,128)} %get-tuple-element.38), channel_id=1, source_target_pairs={{1,0},{2,1},{3,2},{5,4},{6,5},{7,6},{9,8},{10,9},{11,10},{13,12},{... | collective-permute-start | bytes 1179656 | tf_op jit(solution)/shard_map/ppermute | solution.py:20
  7.0 108.4 %collective-permute-start.2 = (f32[4,1,48,512]{3,0,1,2:T(4,128)}, f32[4,1,48,512]{3,0,1,2:T(4,128)}, u32[]{:S(2)}, u32[]{:S(2)}) collective-permute-start(f32[4,1,48,512]{3,0,1,2:T(4,128)} %get-tuple-element.39), channel_id=1, source_target_pairs={{0,1},{1,2},{2,3},{4,5},{5,6},{6,7},{8,9},{9,10},{10,11},{12,13},{... | collective-permute-start | bytes 1179656 | tf_op jit(solution)/shard_map/ppermute | solution.py:17
  10.8 90.0 %collective-permute-start.1 = (f32[1,48,128]{2,1,0:T(8,128)S(1)}, f32[1,48,128]{2,1,0:T(8,128)S(1)}, u32[]{:S(2)}, u32[]{:S(2)}) collective-permute-start(f32[1,48,128]{2,1,0:T(8,128)S(1)} %slice.144), channel_id=1, source_target_pairs={{0,1},{1,2},{2,3},{4,5},{5,6},{6,7},{8,9},{9,10},{10,11},{12,13},{... | collective-permute-start | bytes 73736 | tf_op jit(solution)/shard_map/ppermute | solution.py:28
  21.1 40.6 %copy-start.19 = (f32[8,48,128]{2,1,0:T(8,128)S(1)}, f32[8,48,128]{2,1,0:T(8,128)}, u32[]{:S(2)}) copy-start(f32[8,48,128]{2,1,0:T(8,128)} %param.21) | copy-start | bytes 589828
  42.5 41.4 %copy-start.20 = (f32[4,8,512]{2,1,0:T(8,128)S(1)}, f32[4,8,512]{2,1,0:T(8,128)}, u32[]{:S(2)}) copy-start(f32[4,8,512]{2,1,0:T(8,128)} %param.14) | copy-start | bytes 196612
  42.5 47.6 %slice-start = ((f32[4,8,48,512]{3,0,1,2:T(4,128)}), f32[4,8,47,512]{3,0,1,2:T(4,128)S(1)}, s32[]{:S(2)}) async-start(f32[4,8,48,512]{3,0,1,2:T(4,128)} %copy-done.2), calls=%async_computation | async-start | bytes 6160384 | tf_op jit(solution)/shard_map/slice | solution.py:34
  90.1 6.1 %copy-start.9 = (f32[8,48,512]{2,1,0:T(8,128)S(1)}, f32[8,48,512]{2,1,0:T(8,128)}, u32[]{:S(2)}) copy-start(f32[8,48,512]{2,1,0:T(8,128)} %copy-done.8) | copy-start | bytes 2359300
  96.6 3.7 %copy-start.15 = (f32[8,48,512]{2,1,0:T(8,128)S(1)}, f32[8,48,512]{2,1,0:T(8,128)}, u32[]{:S(2)}) copy-start(f32[8,48,512]{2,1,0:T(8,128)} %get-tuple-element.45) | copy-start | bytes 2359300
  96.6 18.7 %copy-start.7 = (f32[4,8,48,511]{3,0,1,2:T(4,128)S(1)}, f32[4,8,48,511]{3,0,1,2:T(4,128)}, u32[]{:S(2)}) copy-start(f32[4,8,48,511]{3,0,1,2:T(4,128)} %get-tuple-element.37) | copy-start | bytes 9418756
  97.9 17.5 %copy-start.11 = (f32[4,8,48,1]{3,0,1,2:T(4,128)S(1)}, f32[4,8,48,1]{3,0,1,2:T(4,128)}, u32[]{:S(2)}) copy-start(f32[4,8,48,1]{3,0,1,2:T(4,128)} %get-tuple-element.34) | copy-start | bytes 18436
  97.9 17.5 %copy-start.12 = (f32[4,8,48,1]{3,0,1,2:T(4,128)S(1)}, f32[4,8,48,1]{3,0,1,2:T(4,128)}, u32[]{:S(2)}) copy-start(f32[4,8,48,1]{3,0,1,2:T(4,128)} %get-tuple-element.35) | copy-start | bytes 18436
  98.4 17.0 %copy-start.6 = (f32[4,8,48,511]{3,0,1,2:T(4,128)S(1)}, f32[4,8,48,511]{3,0,1,2:T(4,128)}, u32[]{:S(2)}) copy-start(f32[4,8,48,511]{3,0,1,2:T(4,128)} %get-tuple-element.36) | copy-start | bytes 9418756
  98.9 15.3 %slice-start.2 = ((f32[8,48,512]{2,1,0:T(8,128)}), f32[7,48,512]{2,1,0:T(8,128)S(1)}, s32[]{:S(2)}) async-start(f32[8,48,512]{2,1,0:T(8,128)} %all_gather.16), calls=%async_computation.2 | async-start | bytes 1376256 | tf_op jit(solution)/shard_map/slice | solution.py:112
  99.4 16.0 %copy-start.5 = (f32[4,8,48,512]{3,0,1,2:T(4,128)S(1)}, f32[4,8,48,512]{3,0,1,2:T(4,128)}, u32[]{:S(2)}) copy-start(f32[4,8,48,512]{3,0,1,2:T(4,128)} %copy-done.4) | copy-start | bytes 9437188
  100.3 15.1 %slice-start.1 = ((f32[4,8,48,512]{3,0,1,2:T(4,128)}), f32[4,8,47,512]{3,0,1,2:T(4,128)S(1)}, s32[]{:S(2)}) async-start(f32[4,8,48,512]{3,0,1,2:T(4,128)} %copy-done.4), calls=%async_computation.1 | async-start | bytes 6160384 | tf_op jit(solution)/shard_map/slice | solution.py:38
  100.8 14.6 %copy-start.3 = (f32[4,8,48,512]{3,0,1,2:T(4,128)S(1)}, f32[4,8,48,512]{3,0,1,2:T(4,128)}, u32[]{:S(2)}) copy-start(f32[4,8,48,512]{3,0,1,2:T(4,128)} %copy-done.2) | copy-start | bytes 9437188
  115.4 10.3 %copy-start.21 = (s32[8,512]{1,0:T(8,128)S(1)}, s32[8,512]{1,0:T(8,128)}, u32[]{:S(2)}) copy-start(s32[8,512]{1,0:T(8,128)} %param.17) | copy-start | bytes 49156
  115.5 10.3 %copy-start.22 = (f32[4,22]{1,0:T(4,128)S(1)}, f32[4,22]{1,0:T(4,128)}, u32[]{:S(2)}) copy-start(f32[4,22]{1,0:T(4,128)} %param.18) | copy-start | bytes 1060
  130.2 7.8 %collective-permute-start.3 = (f32[4,1,48,512]{3,0,1,2:T(4,128)S(1)}, f32[4,1,48,512]{3,0,1,2:T(4,128)S(1)}, u32[]{:S(2)}, u32[]{:S(2)}) collective-permute-start(f32[4,1,48,512]{3,0,1,2:T(4,128)S(1)} %get-tuple-element.32), channel_id=1, source_target_pairs={{1,0},{2,1},{3,2},{5,4},{6,5},{7,6},{9,8},{10,9},{11,10},{13,12},{... | collective-permute-start | bytes 1179656 | tf_op jit(solution)/shard_map/ppermute | solution.py:20
  131.5 6.5 %collective-permute-start.4 = (f32[4,1,48,512]{3,0,1,2:T(4,128)S(1)}, f32[4,1,48,512]{3,0,1,2:T(4,128)S(1)}, u32[]{:S(2)}, u32[]{:S(2)}) collective-permute-start(f32[4,1,48,512]{3,0,1,2:T(4,128)S(1)} %get-tuple-element.33), channel_id=1, source_target_pairs={{0,1},{1,2},{2,3},{4,5},{5,6},{6,7},{8,9},{9,10},{10,11},{12,13},{... | collective-permute-start | bytes 1179656 | tf_op jit(solution)/shard_map/ppermute | solution.py:17
  147.1 3.5 %copy-start.1 = (f32[8,8,8]{2,1,0:T(8,128)S(1)}, f32[8,8,8]{2,1,0:T(8,128)}, u32[]{:S(2)}) copy-start(f32[8,8,8]{2,1,0:T(8,128)} %param.15) | copy-start | bytes 6148
  (7 other events, 14.3 us)
where the time goes:
time: 152 us; the launch traced here: 151 us
  blocking collectives  75.9 us (50%)
  other arithmetic  31.4 us (21%)
  local copies, waits for them, and re-layouts  28.1 us (18%)
  starting transfers between devices  13.4 us (9%)
    all_gather x1, blocking collectives, on_device(): lax.all_gather(zonal_courant, 'tracer', axis=2, tiled=True)  20 us
    sub x2, other arithmetic, advance(): tracer_now - (flux_east - flux_west) - (flux_north - flux_south)  19.4 us
    all_gather x1, blocking collectives, on_device(): lax.all_gather(meridional_courant, 'tracer', axis=2, tiled=True)  19.1 us
    all_gather x1, blocking collectives, on_device(): lax.all_gather(vertical_diffusion, 'tracer', axis=2, tiled=True)  17.4 us
    all_gather x1, blocking collectives, on_device(): lax.all_gather(south_row, 'tracer', axis=2, tiled=True)  13.4 us
    unnamed x49, local copies, waits for them, and re-layouts  9.99 us
    slice x4, local copies, waits for them, and re-layouts, sideways(): return (jnp.roll(tracer_now, 1, axis=3), jnp.roll(tracer_now, -1, axis=3))  9.62 us
    mul x2, other arithmetic, vertical_mixing(): flux_up = mixing * (tracer_now - upper_level) * open_top  7.61 us
  transfers between devices with their start and end apart: 5, of which 0 were waited for; matrix products, arithmetic and copies ran while one was open for 18% of the time, Pallas kernels for 0%

commit v1 on v0

--- a/solution.py
+++ b/solution.py
@@ -1,6 +1,9 @@
+import functools
 import jax
 import jax.numpy as jnp
 from jax import lax
+from jax.experimental import pallas as pl
+from jax.experimental.pallas import tpu as pltpu
 from jax.sharding import PartitionSpec as P
 
 STEPS = 2
@@ -122,6 +125,352 @@
     return (tracer_field, emission)
 
 
+LINE = 4
+
+
+def fits_fused(mesh):
+    return mesh.shape["tracer"] == LINE
+
+
+def piece(c, rows):
+    if isinstance(c, int) and c == 0:
+        return pl.ds(0, 4)
+    if isinstance(c, int) and c == rows - 1:
+        return pl.ds(3 * c + 1, 2)
+    return pl.ds(3 * c + 1, 3)
+
+
+def mirror(z):
+    return z + 1 - 2 * lax.rem(z, 2)
+
+
+def transport_row(weather, emission, source, target, row, target_row, north, south, zonal):
+    tracers, _, levels, lons = source.shape
+    top = lax.broadcasted_iota(jnp.int32, (levels, lons), 0) == levels - 1
+
+    def item(index):
+        return jnp.concatenate([weather[j, index] for j in range(LINE)], axis=1)
+
+    def one(k, carry):
+        q, q_north, q_south = source[k, row], source[k, row + 1], source[k, row - 1]
+        u, d, m, m_south = item(zonal), item(zonal + 1), item(north), item(south)
+        flux_east = u * jnp.where(u > 0.0, q, pltpu.roll(q, lons - 1, 1))
+        flux_north = m * jnp.where(m > 0.0, q, q_north)
+        flux_south = m_south * jnp.where(m_south > 0.0, q_south, q)
+        flux_up = d * (q - jnp.where(top, q, pltpu.roll(q, levels - 1, 0)))
+        result = q - (flux_east - pltpu.roll(flux_east, 1, 1)) - (flux_north - flux_south)
+        result = result - (flux_up - pltpu.roll(flux_up, 1, 0))
+        target[k, target_row] = result
+        target[k, target_row, 0:1, :] = result[0:1] + emission[k, pl.ds(row - 1, 1), :]
+        return carry
+
+    lax.fori_loop(0, tracers, one, 0)
+
+
+def window_kernel(
+    bands,
+    tile_index,
+    region_sigma,
+    region_map,
+    prior_tiles,
+    state,
+    control,
+    zonal_courant,
+    meridional_courant,
+    vertical_diffusion,
+    final,
+    emission,
+    first,
+    second,
+    weather,
+    increments,
+    own_sem,
+    state_sem,
+    piece_send,
+    piece_recv,
+    relay_send,
+    control_sem,
+    control_send,
+    control_recv,
+    edge_send,
+    edge_recv,
+):
+    z, b = lax.axis_index("tracer"), lax.axis_index("band")
+    tracers, rows, levels, lons = state.shape
+    regions = region_sigma.shape[1]
+    halo_item, closed_item = 3 * rows, 3 * rows + 1
+    near, far = mirror(z), jnp.where(z < 2, 2, 1)
+    beyond, beyond_next = 3 - z, mirror(3 - z)
+    inner = jnp.logical_and(z > 0, z < LINE - 1)
+    has_south, has_north = b > 0, b < bands - 1
+
+    def send(src, dst, send_sem, recv_sem, **where):
+        return pltpu.make_async_remote_copy(
+            src_ref=src, dst_ref=dst, send_sem=send_sem, recv_sem=recv_sem,
+            device_id=where, device_id_type=pl.DeviceIdType.MESH,
+        )
+
+    def own_item(c, index, array, row):
+        return pltpu.make_async_copy(array.at[row], weather.at[z, index], own_sem.at[c])
+
+    def start_own(c):
+        row = (c + rows - 1) % rows
+        index = 3 * c + 1
+        if c == 0:
+            own_item(c, 0, meridional_courant, rows - 2).start()
+        if c < rows - 1:
+            own_item(c, index, meridional_courant, row).start()
+            index += 1
+        own_item(c, index, zonal_courant, row).start()
+        own_item(c, index + 1, vertical_diffusion, row).start()
+
+    for c in range(rows):
+        start_own(c)
+    load_state = pltpu.make_async_copy(state, first.at[:, pl.ds(1, rows)], state_sem.at[0])
+    load_state.start()
+    own_rows = pl.ds(pl.multiple_of(b * rows, rows), rows)
+    load_control = pltpu.make_async_copy(control, increments.at[:, own_rows], control_sem.at[0])
+    load_control.start()
+
+    barrier = pltpu.get_barrier_semaphore()
+    for step in range(1, LINE):
+        pl.semaphore_signal(
+            barrier, inc=1, device_id={"tracer": lax.rem(z + step, LINE)}, device_id_type=pl.DeviceIdType.MESH
+        )
+    for step in range(1, bands):
+        pl.semaphore_signal(
+            barrier, inc=1, device_id={"band": lax.rem(b + step, bands)}, device_id_type=pl.DeviceIdType.MESH
+        )
+    pl.semaphore_wait(barrier, LINE - 1 + bands - 1)
+
+    def piece_copy(c, owner, target, sems, slot):
+        part = weather.at[owner, piece(c, rows)]
+        return send(part, part, sems.at[c, slot], piece_recv.at[c, owner], tracer=target)
+
+    for c in range(rows):
+        part = weather.at[z, piece(c, rows)]
+        pltpu.make_async_copy(part, part, own_sem.at[c]).wait()
+        piece_copy(c, z, near, piece_send, 0).start()
+        piece_copy(c, z, far, piece_send, 1).start()
+
+    def edge_copy(slot):
+        src, dst, step = (
+            (state.at[:, rows - 1], first.at[:, 0], 1),
+            (state.at[:, 0], first.at[:, rows + 1], -1),
+            (second.at[:, rows], second.at[:, 0], 1),
+            (second.at[:, 1], second.at[:, rows + 1], -1),
+            (weather.at[:, 1], weather.at[:, halo_item], 1),
+        )[slot]
+        target = jnp.clip(b + step, 0, bands - 1)
+        return send(src, dst, edge_send.at[slot], edge_recv.at[slot], band=target)
+
+    def control_copy(step):
+        return send(
+            control, increments.at[:, own_rows], control_send.at[step], control_recv.at[b],
+            band=lax.rem(b + step, bands),
+        )
+
+    for step in range(1, bands):
+        control_copy(step).start()
+
+    @pl.when(has_north)
+    def _():
+        edge_copy(0).start()
+
+    @pl.when(has_south)
+    def _():
+        edge_copy(1).start()
+
+    zero_row = jnp.zeros((levels, lons), jnp.float32)
+    zero_item = jnp.zeros((levels, lons // LINE), jnp.float32)
+    for j in range(LINE):
+        weather[j, closed_item] = zero_item
+
+    @pl.when(b == 0)
+    def _():
+        for j in range(LINE):
+            weather[j, halo_item] = zero_item
+        for k in range(tracers):
+            first[k, 0] = zero_row
+            second[k, 0] = zero_row
+
+    @pl.when(b == bands - 1)
+    def _():
+        for k in range(tracers):
+            first[k, rows + 1] = zero_row
+            second[k, rows + 1] = zero_row
+
+    load_control.wait()
+    for step in range(1, bands):
+        source_band = lax.rem(b + step, bands)
+        part = increments.at[:, pl.ds(pl.multiple_of(source_band * rows, rows), rows)]
+        pltpu.make_async_copy(part, part, control_recv.at[source_band]).wait()
+    region = region_map[...]
+    for k in range(tracers):
+        field = jnp.zeros((rows, lons), jnp.float32)
+        for j in range(bands):
+            tile = prior_tiles[tile_index[b, j]]
+            for row in range(rows):
+                field = field + tile[:, row : row + 1] * increments[k, j * rows + row : j * rows + row + 1, :]
+        sigma = jnp.zeros((rows, lons), jnp.float32)
+        for r in range(regions):
+            sigma = jnp.where(region == r, region_sigma[k, r], sigma)
+        emission[k] = sigma * field
+
+    load_state.wait()
+
+    @pl.when(has_south)
+    def _():
+        pltpu.make_async_copy(first.at[:, 0], first.at[:, 0], edge_recv.at[0]).wait()
+
+    @pl.when(has_north)
+    def _():
+        pltpu.make_async_copy(first.at[:, rows + 1], first.at[:, rows + 1], edge_recv.at[1]).wait()
+
+    def arrive(c):
+        for slot, owner in enumerate((beyond, beyond_next)):
+            part = weather.at[owner, piece(c, rows)]
+            pltpu.make_async_copy(part, part, piece_recv.at[c, owner]).wait()
+
+            @pl.when(inner)
+            def _():
+                piece_copy(c, owner, near, relay_send, slot).start()
+
+        part = weather.at[near, piece(c, rows)]
+        pltpu.make_async_copy(part, part, piece_recv.at[c, near]).wait()
+
+    last_north = jnp.where(has_north, 1, closed_item)
+    one_step = functools.partial(transport_row, weather, emission, first, second)
+    two_step = functools.partial(transport_row, weather, emission, second, final)
+
+    def second_step(row, north, south, zonal):
+        two_step(row + 1, row, north, south, zonal)
+
+    arrive(0)
+
+    @pl.when(has_north)
+    def _():
+        edge_copy(4).start()
+
+    one_step(rows, rows, last_north, 0, 2)
+
+    @pl.when(has_north)
+    def _():
+        edge_copy(2).start()
+
+    arrive(1)
+
+    @pl.when(has_south)
+    def _():
+        pltpu.make_async_copy(weather.at[:, halo_item], weather.at[:, halo_item], edge_recv.at[4]).wait()
+
+    one_step(1, 1, 4, halo_item, 5)
+
+    @pl.when(has_south)
+    def _():
+        edge_copy(3).start()
+        pltpu.make_async_copy(second.at[:, 0], second.at[:, 0], edge_recv.at[2]).wait()
+
+    def middle(c, carry):
+        arrive(c)
+        one_step(c, c, 3 * c + 1, 3 * c - 2, 3 * c + 2)
+        second_step(c - 2, 3 * c - 2, jnp.where(c == 2, halo_item, 3 * c - 5), 3 * c - 1)
+        return carry
+
+    lax.fori_loop(2, rows - 1, middle, 0)
+
+    c = rows - 1
+    arrive(c)
+    one_step(c, c, 0, 3 * c - 2, 3 * c + 1)
+    second_step(c - 2, 3 * c - 2, 3 * c - 5, 3 * c - 1)
+
+    @pl.when(has_north)
+    def _():
+        pltpu.make_async_copy(second.at[:, rows + 1], second.at[:, rows + 1], edge_recv.at[3]).wait()
+
+    second_step(rows - 2, 0, 3 * c - 2, 3 * c + 1)
+    second_step(rows - 1, last_north, 0, 2)
+
+    for c in range(rows):
+        piece_copy(c, z, near, piece_send, 0).wait_send()
+        piece_copy(c, z, far, piece_send, 1).wait_send()
+
+        @pl.when(inner)
+        def _():
+            piece_copy(c, beyond, near, relay_send, 0).wait_send()
+            piece_copy(c, beyond_next, near, relay_send, 1).wait_send()
+
+    for step in range(1, bands):
+        control_copy(step).wait_send()
+
+    @pl.when(has_north)
+    def _():
+        for slot in (0, 2, 4):
+            edge_copy(slot).wait_send()
+
+    @pl.when(has_south)
+    def _():
+        for slot in (1, 3):
+            edge_copy(slot).wait_send()
+
+
+def on_device_fused(
+    tracer_state,
+    control,
+    prior_tiles,
+    tile_index,
+    region_map,
+    region_sigma,
+    zonal_courant,
+    meridional_courant,
+    vertical_diffusion,
+):
+    tracers, rows, levels, lons = tracer_state.shape
+    bands = lax.axis_size("band")
+    dma = pltpu.SemaphoreType.DMA
+    smem = pl.BlockSpec(memory_space=pltpu.SMEM)
+    vmem = pl.BlockSpec(memory_space=pltpu.VMEM)
+    anywhere = pl.BlockSpec(memory_space=pl.ANY)
+    return pl.pallas_call(
+        functools.partial(window_kernel, bands),
+        out_shape=(
+            jax.ShapeDtypeStruct(tracer_state.shape, jnp.float32),
+            jax.ShapeDtypeStruct(control.shape, jnp.float32),
+        ),
+        in_specs=[smem, smem, vmem, vmem] + [anywhere] * 5,
+        out_specs=(vmem, vmem),
+        scratch_shapes=[
+            pltpu.VMEM((tracers, rows + 2, levels, lons), jnp.float32),
+            pltpu.VMEM((tracers, rows + 2, levels, lons), jnp.float32),
+            pltpu.VMEM((LINE, 3 * rows + 2, levels, lons // LINE), jnp.float32),
+            pltpu.VMEM((tracers, bands * rows, lons), jnp.float32),
+            dma((rows,)),
+            dma((1,)),
+            dma((rows, 2)),
+            dma((rows, LINE)),
+            dma((rows, 2)),
+            dma((1,)),
+            dma((bands,)),
+            dma((bands,)),
+            dma((5,)),
+            dma((5,)),
+        ],
+        compiler_params=pltpu.CompilerParams(
+            collective_id=0, has_side_effects=True, vmem_limit_bytes=40 * 1024 * 1024
+        ),
+    )(
+        tile_index,
+        region_sigma,
+        region_map,
+        prior_tiles,
+        tracer_state,
+        control,
+        zonal_courant,
+        meridional_courant,
+        vertical_diffusion,
+    )
+
+
 def solution(mesh):
     in_specs = (
         P(("inv", "tracer"), "band", None, None),
@@ -135,6 +484,7 @@
         P(("inv", "band"), None, "tracer"),
     )
     out_specs = (P(("inv", "tracer"), "band", None, None), P(("inv", "tracer"), "band", None))
+    body = on_device_fused if fits_fused(mesh) else on_device
     return jax.shard_map(
-        on_device, mesh=mesh, in_specs=in_specs, out_specs=out_specs, check_vma=False
-    )
+        body, mesh=mesh, in_specs=in_specs, out_specs=out_specs, check_vma=False
+    )

time: 152 us -> 61.5 us (0.40)
  blocking collectives: 75.9 us -> 0 us
  Pallas kernels: 0 us -> 49.8 us
  other arithmetic: 31.4 us -> 0 us
  local copies, waits for them, and re-layouts: 28.1 us -> 10.6 us
  starting transfers between devices: 13.4 us -> 0 us
    all_gather x5 -> x0, blocking collectives: 75.9 us -> none  [the longest x1 20 us: on_device(): lax.all_gather(zonal_courant, 'tracer', axis=2, tiled=True)]
    pallas_call x0 -> x1, Pallas kernels: none -> 49.8 us  [on_device_fused(): pl.pallas_call(functools.partial(window_kernel, bands), out_shape=(jax.Sh...]
    sub x2 -> x0, other arithmetic: 19.4 us -> none  [advance(): tracer_now - (flux_east - flux_west) - (flux_north - flux_south)]
    ppermute x5 -> x0, starting transfers between devices: 13.4 us -> none  [the longest x2 7.07 us: padded_2(): lax.ppermute(lax.slice_in_dim(block, block.shape[dim] - width, None, axis...]
    slice x16 -> x0, local copies, waits for them, and re-layouts: 12.4 us -> none  [the longest x4 9.62 us: sideways(): return (jnp.roll(tracer_now, 1, axis=3), jnp.roll(tracer_now, -1, axis=3))]
    mul x2 -> x0, other arithmetic: 7.61 us -> none  [vertical_mixing(): flux_up = mixing * (tracer_now - upper_level) * open_top]
    max x4 -> x0, other arithmetic: 4.36 us -> none  [the longest x1 2.5 us: advance(): jnp.maximum(meridional, 0.0) * tracer_now]
    min x4 -> x0, local copies, waits for them, and re-layouts: 1.84 us -> none  [the longest x1 0.46 us: advance(): jnp.minimum(zonal_west, 0.0) * tracer_now]
  transfers between devices with their start and end apart: 5 -> 0, of which waited for: 0 -> 0; matrix products, arithmetic and copies ran while one was open for 18% -> 0% of each run, Pallas kernels for 0% -> 0%
where the time goes in v1:
time: 61.5 us; the launch traced here: 61 us
  Pallas kernels  49.8 us (81%)
  local copies, waits for them, and re-layouts  10.6 us (17%)
  between operations  0.66 us (1%)
    pallas_call x1, Pallas kernels, on_device_fused(): pl.pallas_call(functools.partial(window_kernel, bands), out_shape=(jax.Sh...  49.8 us
    unnamed x20, local copies, waits for them, and re-layouts  10.6 us

profile of v1, /device:TPU:0, one launch (start us, length us, event | category | flops | bytes accessed | tf_op | source)
XLA Modules:
  0.0 61.0 jit_solution(17710354334168087207)
XLA Ops:
  0.6 0.0 copy-start
  0.6 1.9 %copy-done = f32[4,8,48,512]{3,2,1,0:T(8,128)S(1)} copy-done((f32[4,8,48,512]{3,2,1,0:T(8,128)S(1)}, f32[4,8,48,512]{3,2,1,0:T(8,128)}, u32[]{:S(2)}) %copy-start) | copy-done | bytes 3145752
  2.5 0.0 copy-start.1
  2.5 0.9 %copy-done.1 = f32[8,48,128]{2,1,0:T(8,128)S(1)} copy-done((f32[8,48,128]{2,1,0:T(8,128)S(1)}, f32[8,48,128]{2,1,0:T(8,128)}, u32[]{:S(2)}) %copy-start.1) | copy-done | bytes 196632
  3.5 0.0 copy-start.2
  3.5 0.9 %copy-done.2 = f32[8,48,128]{2,1,0:T(8,128)S(1)} copy-done((f32[8,48,128]{2,1,0:T(8,128)S(1)}, f32[8,48,128]{2,1,0:T(8,128)}, u32[]{:S(2)}) %copy-start.2) | copy-done | bytes 196632
  4.4 0.0 copy-start.3
  4.4 0.9 %copy-done.3 = f32[8,48,128]{2,1,0:T(8,128)S(1)} copy-done((f32[8,48,128]{2,1,0:T(8,128)S(1)}, f32[8,48,128]{2,1,0:T(8,128)}, u32[]{:S(2)}) %copy-start.3) | copy-done | bytes 196632
  5.3 0.0 copy-start.4
  5.3 0.8 %copy-done.4 = f32[4,8,512]{2,1,0:T(8,128)S(1)} copy-done((f32[4,8,512]{2,1,0:T(8,128)S(1)}, f32[4,8,512]{2,1,0:T(8,128)}, u32[]{:S(2)}) %copy-start.4) | copy-done | bytes 65560
  6.1 0.0 copy-start.5
  6.1 0.8 %copy-done.5 = f32[8,8,8]{2,1,0:T(8,128)S(1)} copy-done((f32[8,8,8]{2,1,0:T(8,128)S(1)}, f32[8,8,8]{2,1,0:T(8,128)}, u32[]{:S(2)}) %copy-start.5) | copy-done | bytes 2072
  6.9 0.0 copy-start.6
  6.9 0.7 %copy-done.6 = s32[8,512]{1,0:T(8,128)S(1)} copy-done((s32[8,512]{1,0:T(8,128)S(1)}, s32[8,512]{1,0:T(8,128)}, u32[]{:S(2)}) %copy-start.6) | copy-done | bytes 16408
  7.6 0.0 copy-start.7
  7.6 0.7 %copy-done.7 = s32[4,4]{1,0:T(4,128)S(1)} copy-done((s32[4,4]{1,0:T(4,128)S(1)}, s32[4,4]{1,0:T(4,128)}, u32[]{:S(2)}) %copy-start.7) | copy-done | bytes 88
  8.3 0.0 copy-start.8
  8.3 0.7 %copy-done.8 = f32[4,22]{1,0:T(4,128)S(1)} copy-done((f32[4,22]{1,0:T(4,128)S(1)}, f32[4,22]{1,0:T(4,128)}, u32[]{:S(2)}) %copy-start.8) | copy-done | bytes 376
  9.0 49.8 %shard_map.104 = (f32[4,8,48,512]{3,2,1,0:T(8,128)S(1)}, f32[4,8,512]{2,1,0:T(8,128)S(1)}) custom-call(s32[4,4]{1,0:T(4,128)S(1)} %copy-done.7, f32[4,22]{1,0:T(4,128)S(1)} %copy-done.8, s32[8,512]{1,0:T(8,128)S(1)} %copy-done.6, f32[8,8,8]{2,1,0:T(8,128)S(1)} %copy-done.5, f32[4,8,48,512]{3,2,1,0:T(8,128)S(1)} %copy-done, f32[4,8,512]{2,1,0:T(8,128)S(1)} %copy-done.4, ...), custom_call_target="tpu_custom_call" | custom-call | tf_op jit(solution)/shard_map/pallas_call | solution.py:434
  58.8 1.7 %copy.13 = f32[4,8,48,512]{3,2,1,0:T(8,128)} copy(f32[4,8,48,512]{3,2,1,0:T(8,128)S(1)} %get-tuple-element.4) | data formatting | bytes 6291456
  60.4 0.6 %copy.14 = f32[4,8,512]{2,1,0:T(8,128)} copy(f32[4,8,512]{2,1,0:T(8,128)S(1)} %get-tuple-element.5) | data formatting | bytes 131072
Async XLA Ops:
  0.6 1.9 %copy-start = (f32[4,8,48,512]{3,2,1,0:T(8,128)S(1)}, f32[4,8,48,512]{3,2,1,0:T(8,128)}, u32[]{:S(2)}) copy-start(f32[4,8,48,512]{3,2,1,0:T(8,128)} %state.1) | copy-start | bytes 9437188
  2.5 0.9 %copy-start.1 = (f32[8,48,128]{2,1,0:T(8,128)S(1)}, f32[8,48,128]{2,1,0:T(8,128)}, u32[]{:S(2)}) copy-start(f32[8,48,128]{2,1,0:T(8,128)} %zonal_courant.1) | copy-start | bytes 589828
  3.5 0.9 %copy-start.2 = (f32[8,48,128]{2,1,0:T(8,128)S(1)}, f32[8,48,128]{2,1,0:T(8,128)}, u32[]{:S(2)}) copy-start(f32[8,48,128]{2,1,0:T(8,128)} %meridional_courant.1) | copy-start | bytes 589828
  4.4 0.9 %copy-start.3 = (f32[8,48,128]{2,1,0:T(8,128)S(1)}, f32[8,48,128]{2,1,0:T(8,128)}, u32[]{:S(2)}) copy-start(f32[8,48,128]{2,1,0:T(8,128)} %vertical_diffusion.1) | copy-start | bytes 589828
  5.3 0.8 %copy-start.4 = (f32[4,8,512]{2,1,0:T(8,128)S(1)}, f32[4,8,512]{2,1,0:T(8,128)}, u32[]{:S(2)}) copy-start(f32[4,8,512]{2,1,0:T(8,128)} %control.1) | copy-start | bytes 196612
  6.1 0.8 %copy-start.5 = (f32[8,8,8]{2,1,0:T(8,128)S(1)}, f32[8,8,8]{2,1,0:T(8,128)}, u32[]{:S(2)}) copy-start(f32[8,8,8]{2,1,0:T(8,128)} %prior_tiles.1) | copy-start | bytes 6148
  6.9 0.7 %copy-start.6 = (s32[8,512]{1,0:T(8,128)S(1)}, s32[8,512]{1,0:T(8,128)}, u32[]{:S(2)}) copy-start(s32[8,512]{1,0:T(8,128)} %region_map.1) | copy-start | bytes 49156
  7.6 0.7 %copy-start.7 = (s32[4,4]{1,0:T(4,128)S(1)}, s32[4,4]{1,0:T(4,128)}, u32[]{:S(2)}) copy-start(s32[4,4]{1,0:T(4,128)} %tile_index.1) | copy-start | bytes 196
  8.3 0.7 %copy-start.8 = (f32[4,22]{1,0:T(4,128)S(1)}, f32[4,22]{1,0:T(4,128)}, u32[]{:S(2)}) copy-start(f32[4,22]{1,0:T(4,128)} %region_sigma.1) | copy-start | bytes 1060

commit v2 on v1

--- a/solution.py
+++ b/solution.py
@@ -169,10 +169,10 @@
 
 def window_kernel(
     bands,
-    tile_index,
-    region_sigma,
-    region_map,
-    prior_tiles,
+    tile_index_hbm,
+    region_sigma_hbm,
+    region_map_hbm,
+    prior_tiles_hbm,
     state,
     control,
     zonal_courant,
@@ -184,6 +184,11 @@
     second,
     weather,
     increments,
+    tile_index,
+    region_sigma,
+    region_map,
+    prior_tiles,
+    table_sem,
     own_sem,
     state_sem,
     piece_send,
@@ -199,8 +204,7 @@
     tracers, rows, levels, lons = state.shape
     regions = region_sigma.shape[1]
     halo_item, closed_item = 3 * rows, 3 * rows + 1
-    near, far = mirror(z), jnp.where(z < 2, 2, 1)
-    beyond, beyond_next = 3 - z, mirror(3 - z)
+    near, far, opposite = mirror(z), jnp.where(z < 2, 2, 1), LINE - 1 - z
     inner = jnp.logical_and(z > 0, z < LINE - 1)
     has_south, has_north = b > 0, b < bands - 1
 
@@ -231,6 +235,13 @@
     own_rows = pl.ds(pl.multiple_of(b * rows, rows), rows)
     load_control = pltpu.make_async_copy(control, increments.at[:, own_rows], control_sem.at[0])
     load_control.start()
+    tables = (
+        (tile_index_hbm, tile_index), (region_sigma_hbm, region_sigma),
+        (region_map_hbm, region_map), (prior_tiles_hbm, prior_tiles),
+    )
+    load_tables = [pltpu.make_async_copy(src, dst, table_sem.at[i]) for i, (src, dst) in enumerate(tables)]
+    for load in load_tables:
+        load.start()
 
     barrier = pltpu.get_barrier_semaphore()
     for step in range(1, LINE):
@@ -253,6 +264,10 @@
         piece_copy(c, z, near, piece_send, 0).start()
         piece_copy(c, z, far, piece_send, 1).start()
 
+        @pl.when(jnp.logical_not(inner))
+        def _():
+            piece_copy(c, z, opposite, relay_send, 0).start()
+
     def edge_copy(slot):
         src, dst, step = (
             (state.at[:, rows - 1], first.at[:, 0], 1),
@@ -301,20 +316,28 @@
             second[k, rows + 1] = zero_row
 
     load_control.wait()
+    for load in load_tables:
+        load.wait()
     for step in range(1, bands):
         source_band = lax.rem(b + step, bands)
         part = increments.at[:, pl.ds(pl.multiple_of(source_band * rows, rows), rows)]
         pltpu.make_async_copy(part, part, control_recv.at[source_band]).wait()
     region = region_map[...]
+    choice = tile_index[pl.ds(b, 1), :]
+    tiles = []
+    for j in range(bands):
+        tile = jnp.zeros((rows, rows), jnp.float32)
+        for t in range(prior_tiles.shape[0]):
+            tile = jnp.where(choice[:, j : j + 1] == t, prior_tiles[t], tile)
+        tiles.append(tile)
     for k in range(tracers):
         field = jnp.zeros((rows, lons), jnp.float32)
         for j in range(bands):
-            tile = prior_tiles[tile_index[b, j]]
             for row in range(rows):
-                field = field + tile[:, row : row + 1] * increments[k, j * rows + row : j * rows + row + 1, :]
+                field = field + tiles[j][:, row : row + 1] * increments[k, j * rows + row : j * rows + row + 1, :]
         sigma = jnp.zeros((rows, lons), jnp.float32)
         for r in range(regions):
-            sigma = jnp.where(region == r, region_sigma[k, r], sigma)
+            sigma = jnp.where(region == r, region_sigma[k : k + 1, r : r + 1], sigma)
         emission[k] = sigma * field
 
     load_state.wait()
@@ -328,16 +351,18 @@
         pltpu.make_async_copy(first.at[:, rows + 1], first.at[:, rows + 1], edge_recv.at[1]).wait()
 
     def arrive(c):
-        for slot, owner in enumerate((beyond, beyond_next)):
+        def wait_for(owner):
             part = weather.at[owner, piece(c, rows)]
             pltpu.make_async_copy(part, part, piece_recv.at[c, owner]).wait()
 
-            @pl.when(inner)
-            def _():
-                piece_copy(c, owner, near, relay_send, slot).start()
-
-        part = weather.at[near, piece(c, rows)]
-        pltpu.make_async_copy(part, part, piece_recv.at[c, near]).wait()
+        wait_for(opposite)
+
+        @pl.when(inner)
+        def _():
+            piece_copy(c, opposite, near, relay_send, 0).start()
+
+        wait_for(near)
+        wait_for(mirror(opposite))
 
     last_north = jnp.where(has_north, 1, closed_item)
     one_step = functools.partial(transport_row, weather, emission, first, second)
@@ -394,11 +419,7 @@
     for c in range(rows):
         piece_copy(c, z, near, piece_send, 0).wait_send()
         piece_copy(c, z, far, piece_send, 1).wait_send()
-
-        @pl.when(inner)
-        def _():
-            piece_copy(c, beyond, near, relay_send, 0).wait_send()
-            piece_copy(c, beyond_next, near, relay_send, 1).wait_send()
+        piece_copy(c, z, opposite, relay_send, 0).wait_send()
 
     for step in range(1, bands):
         control_copy(step).wait_send()
@@ -428,27 +449,45 @@
     tracers, rows, levels, lons = tracer_state.shape
     bands = lax.axis_size("band")
     dma = pltpu.SemaphoreType.DMA
-    smem = pl.BlockSpec(memory_space=pltpu.SMEM)
     vmem = pl.BlockSpec(memory_space=pltpu.VMEM)
-    anywhere = pl.BlockSpec(memory_space=pl.ANY)
+    hbm = pl.BlockSpec(memory_space=pltpu.HBM)
+    operands = [
+        pltpu.with_memory_space_constraint(operand, pltpu.HBM)
+        for operand in (
+            tile_index,
+            region_sigma,
+            region_map,
+            prior_tiles,
+            tracer_state,
+            control,
+            zonal_courant,
+            meridional_courant,
+            vertical_diffusion,
+        )
+    ]
     return pl.pallas_call(
         functools.partial(window_kernel, bands),
         out_shape=(
             jax.ShapeDtypeStruct(tracer_state.shape, jnp.float32),
             jax.ShapeDtypeStruct(control.shape, jnp.float32),
         ),
-        in_specs=[smem, smem, vmem, vmem] + [anywhere] * 5,
+        in_specs=[hbm] * len(operands),
         out_specs=(vmem, vmem),
         scratch_shapes=[
             pltpu.VMEM((tracers, rows + 2, levels, lons), jnp.float32),
             pltpu.VMEM((tracers, rows + 2, levels, lons), jnp.float32),
             pltpu.VMEM((LINE, 3 * rows + 2, levels, lons // LINE), jnp.float32),
             pltpu.VMEM((tracers, bands * rows, lons), jnp.float32),
+            pltpu.VMEM(tile_index.shape, jnp.int32),
+            pltpu.VMEM(region_sigma.shape, jnp.float32),
+            pltpu.VMEM(region_map.shape, jnp.int32),
+            pltpu.VMEM(prior_tiles.shape, jnp.float32),
+            dma((4,)),
             dma((rows,)),
             dma((1,)),
             dma((rows, 2)),
             dma((rows, LINE)),
-            dma((rows, 2)),
+            dma((rows, 1)),
             dma((1,)),
             dma((bands,)),
             dma((bands,)),
@@ -458,17 +497,7 @@
         compiler_params=pltpu.CompilerParams(
             collective_id=0, has_side_effects=True, vmem_limit_bytes=40 * 1024 * 1024
         ),
-    )(
-        tile_index,
-        region_sigma,
-        region_map,
-        prior_tiles,
-        tracer_state,
-        control,
-        zonal_courant,
-        meridional_courant,
-        vertical_diffusion,
-    )
+    )(*operands)
 
 
 def solution(mesh):

time: 61.5 us -> 53.1 us (0.86)
  local copies, waits for them, and re-layouts: 10.6 us -> 2.3 us
    unnamed x20 -> x2, local copies, waits for them, and re-layouts: 10.6 us -> 2.3 us
where the time goes in v2:
time: 53.1 us; the launch traced here: 53 us
  Pallas kernels  50 us (94%)
  local copies, waits for them, and re-layouts  2.3 us (4%)
  between operations  0.64 us (1%)
    pallas_call x1, Pallas kernels, on_device_fused(): pl.pallas_call(functools.partial(window_kernel, bands), out_shape=(jax.Sh...  50 us
    unnamed x2, local copies, waits for them, and re-layouts  2.3 us

profile of v2, /device:TPU:0, one launch (start us, length us, event | category | flops | bytes accessed | tf_op | source)
XLA Modules:
  0.0 53.0 jit_solution(12585658734904053956)
XLA Ops:
  0.6 50.0 %shard_map.104 = (f32[4,8,48,512]{3,2,1,0:T(8,128)S(1)}, f32[4,8,512]{2,1,0:T(8,128)S(1)}) custom-call(s32[4,4]{1,0:T(4,128)} %tile_index_hbm.1, f32[4,22]{1,0:T(4,128)} %region_sigma_hbm.1, s32[8,512]{1,0:T(8,128)} %region_map_hbm.1, f32[8,8,8]{2,1,0:T(8,128)} %prior_tiles_hbm.1, f32[4,8,48,512]{3,2,1,0:T(8,128)} %state.1, f32[4,8,512]{2,1,0:T(8,128)} %control.1, ...), custom_call_target="tpu_custom_call" | custom-call | tf_op jit(solution)/shard_map/pallas_call | solution.py:468
  50.7 1.7 %copy.13 = f32[4,8,48,512]{3,2,1,0:T(8,128)} copy(f32[4,8,48,512]{3,2,1,0:T(8,128)S(1)} %get-tuple-element.4) | data formatting | bytes 6291456
  52.3 0.6 %copy.14 = f32[4,8,512]{2,1,0:T(8,128)} copy(f32[4,8,512]{2,1,0:T(8,128)S(1)} %get-tuple-element.5) | data formatting | bytes 131072

commit v3 on v2

--- a/solution.py
+++ b/solution.py
@@ -126,10 +126,11 @@
 
 
 LINE = 4
+STRIP = 8
 
 
 def fits_fused(mesh):
-    return mesh.shape["tracer"] == LINE
+    return mesh.shape["tracer"] == LINE and mesh.shape["band"] > 1
 
 
 def piece(c, rows):
@@ -146,22 +147,44 @@
 
 def transport_row(weather, emission, source, target, row, target_row, north, south, zonal):
     tracers, _, levels, lons = source.shape
-    top = lax.broadcasted_iota(jnp.int32, (levels, lons), 0) == levels - 1
-
-    def item(index):
-        return jnp.concatenate([weather[j, index] for j in range(LINE)], axis=1)
+    sublane = lax.broadcasted_iota(jnp.int32, (STRIP, lons), 0)
+    first_sublane, last_sublane = sublane == 0, sublane == STRIP - 1
+    strips = levels // STRIP
 
     def one(k, carry):
-        q, q_north, q_south = source[k, row], source[k, row + 1], source[k, row - 1]
-        u, d, m, m_south = item(zonal), item(zonal + 1), item(north), item(south)
-        flux_east = u * jnp.where(u > 0.0, q, pltpu.roll(q, lons - 1, 1))
-        flux_north = m * jnp.where(m > 0.0, q, q_north)
-        flux_south = m_south * jnp.where(m_south > 0.0, q_south, q)
-        flux_up = d * (q - jnp.where(top, q, pltpu.roll(q, levels - 1, 0)))
-        result = q - (flux_east - pltpu.roll(flux_east, 1, 1)) - (flux_north - flux_south)
-        result = result - (flux_up - pltpu.roll(flux_up, 1, 0))
-        target[k, target_row] = result
-        target[k, target_row, 0:1, :] = result[0:1] + emission[k, pl.ds(row - 1, 1), :]
+        def field(at, strip):
+            return source[k, at, strip * STRIP : (strip + 1) * STRIP, :]
+
+        q = field(row, 0)
+        q_raised = pltpu.roll(q, STRIP - 1, 0)
+        below = jnp.zeros((STRIP, lons), jnp.float32)
+        for strip in range(strips):
+            levels_here = slice(strip * STRIP, (strip + 1) * STRIP)
+
+            def item(index):
+                return jnp.concatenate([weather[j, index, levels_here, :] for j in range(LINE)], axis=1)
+
+            u = item(zonal)
+            flux = u * jnp.where(u > 0.0, q, pltpu.roll(q, lons - 1, 1))
+            result = q - flux + pltpu.roll(flux, 1, 1)
+            m = item(north)
+            result = result - m * jnp.where(m > 0.0, q, field(row + 1, strip))
+            m = item(south)
+            result = result + m * jnp.where(m > 0.0, field(row - 1, strip), q)
+            if strip < strips - 1:
+                q_next = field(row, strip + 1)
+                q_next_raised = pltpu.roll(q_next, STRIP - 1, 0)
+                q_up = jnp.where(last_sublane, q_next_raised, q_raised)
+            else:
+                q_next = q_next_raised = None
+                q_up = jnp.where(last_sublane, q, q_raised)
+            flux = item(zonal + 1) * (q - q_up)
+            lowered = pltpu.roll(flux, 1, 0)
+            result = result - flux + jnp.where(first_sublane, below, lowered)
+            if strip == 0:
+                result = result + jnp.where(first_sublane, emission[k, pl.ds(row - 1, 1), :], 0.0)
+            target[k, target_row, levels_here, :] = result
+            q, q_raised, below = q_next, q_next_raised, lowered
         return carry
 
     lax.fori_loop(0, tracers, one, 0)
@@ -204,7 +227,8 @@
     tracers, rows, levels, lons = state.shape
     regions = region_sigma.shape[1]
     halo_item, closed_item = 3 * rows, 3 * rows + 1
-    near, far, opposite = mirror(z), jnp.where(z < 2, 2, 1), LINE - 1 - z
+    near, far = mirror(z), jnp.where(z < 2, 2, 1)
+    beyond, beyond_next = 3 - z, mirror(3 - z)
     inner = jnp.logical_and(z > 0, z < LINE - 1)
     has_south, has_north = b > 0, b < bands - 1
 
@@ -212,6 +236,16 @@
         return pltpu.make_async_remote_copy(
             src_ref=src, dst_ref=dst, send_sem=send_sem, recv_sem=recv_sem,
             device_id=where, device_id_type=pl.DeviceIdType.MESH,
+        )
+
+    barrier = pltpu.get_barrier_semaphore()
+    for step in range(1, LINE):
+        pl.semaphore_signal(
+            barrier, inc=1, device_id={"tracer": lax.rem(z + step, LINE)}, device_id_type=pl.DeviceIdType.MESH
+        )
+    for step in range(1, bands):
+        pl.semaphore_signal(
+            barrier, inc=1, device_id={"band": lax.rem(b + step, bands)}, device_id_type=pl.DeviceIdType.MESH
         )
 
     def own_item(c, index, array, row):
@@ -243,15 +277,6 @@
     for load in load_tables:
         load.start()
 
-    barrier = pltpu.get_barrier_semaphore()
-    for step in range(1, LINE):
-        pl.semaphore_signal(
-            barrier, inc=1, device_id={"tracer": lax.rem(z + step, LINE)}, device_id_type=pl.DeviceIdType.MESH
-        )
-    for step in range(1, bands):
-        pl.semaphore_signal(
-            barrier, inc=1, device_id={"band": lax.rem(b + step, bands)}, device_id_type=pl.DeviceIdType.MESH
-        )
     pl.semaphore_wait(barrier, LINE - 1 + bands - 1)
 
     def piece_copy(c, owner, target, sems, slot):
@@ -263,10 +288,6 @@
         pltpu.make_async_copy(part, part, own_sem.at[c]).wait()
         piece_copy(c, z, near, piece_send, 0).start()
         piece_copy(c, z, far, piece_send, 1).start()
-
-        @pl.when(jnp.logical_not(inner))
-        def _():
-            piece_copy(c, z, opposite, relay_send, 0).start()
 
     def edge_copy(slot):
         src, dst, step = (
@@ -355,14 +376,14 @@
             part = weather.at[owner, piece(c, rows)]
             pltpu.make_async_copy(part, part, piece_recv.at[c, owner]).wait()
 
-        wait_for(opposite)
-
-        @pl.when(inner)
-        def _():
-            piece_copy(c, opposite, near, relay_send, 0).start()
+        for slot, owner in enumerate((beyond, beyond_next)):
+            wait_for(owner)
+
+            @pl.when(inner)
+            def _():
+                piece_copy(c, owner, near, relay_send, slot).start()
 
         wait_for(near)
-        wait_for(mirror(opposite))
 
     last_north = jnp.where(has_north, 1, closed_item)
     one_step = functools.partial(transport_row, weather, emission, first, second)
@@ -419,7 +440,11 @@
     for c in range(rows):
         piece_copy(c, z, near, piece_send, 0).wait_send()
         piece_copy(c, z, far, piece_send, 1).wait_send()
-        piece_copy(c, z, opposite, relay_send, 0).wait_send()
+
+        @pl.when(inner)
+        def _():
+            piece_copy(c, beyond, near, relay_send, 0).wait_send()
+            piece_copy(c, beyond_next, near, relay_send, 1).wait_send()
 
     for step in range(1, bands):
         control_copy(step).wait_send()
@@ -487,7 +512,7 @@
             dma((1,)),
             dma((rows, 2)),
             dma((rows, LINE)),
-            dma((rows, 1)),
+            dma((rows, 2)),
             dma((1,)),
             dma((bands,)),
             dma((bands,)),

time: 53.1 us -> 51.1 us (0.962)
  Pallas kernels: 50 us -> 48.1 us
    pallas_call x1, Pallas kernels: 50 us -> 48.1 us  [on_device_fused(): pl.pallas_call(functools.partial(window_kernel, bands), out_shape=(jax.Sh...]
where the time goes in v3:
time: 51.1 us; the launch traced here: 51 us
  Pallas kernels  48.1 us (94%)
  local copies, waits for them, and re-layouts  2.3 us (5%)
  between operations  0.64 us (1%)
    pallas_call x1, Pallas kernels, on_device_fused(): pl.pallas_call(functools.partial(window_kernel, bands), out_shape=(jax.Sh...  48.1 us
    unnamed x2, local copies, waits for them, and re-layouts  2.3 us

profile of v3, /device:TPU:0, one launch (start us, length us, event | category | flops | bytes accessed | tf_op | source)
XLA Modules:
  0.0 51.0 jit_solution(13984127512094496504)
XLA Ops:
  0.6 48.1 %shard_map.104 = (f32[4,8,48,512]{3,2,1,0:T(8,128)S(1)}, f32[4,8,512]{2,1,0:T(8,128)S(1)}) custom-call(s32[4,4]{1,0:T(4,128)} %tile_index_hbm.1, f32[4,22]{1,0:T(4,128)} %region_sigma_hbm.1, s32[8,512]{1,0:T(8,128)} %region_map_hbm.1, f32[8,8,8]{2,1,0:T(8,128)} %prior_tiles_hbm.1, f32[4,8,48,512]{3,2,1,0:T(8,128)} %state.1, f32[4,8,512]{2,1,0:T(8,128)} %control.1, ...), custom_call_target="tpu_custom_call" | custom-call | tf_op jit(solution)/shard_map/pallas_call | solution.py:493
  48.7 1.7 %copy.13 = f32[4,8,48,512]{3,2,1,0:T(8,128)} copy(f32[4,8,48,512]{3,2,1,0:T(8,128)S(1)} %get-tuple-element.4) | data formatting | bytes 6291456
  50.4 0.6 %copy.14 = f32[4,8,512]{2,1,0:T(8,128)} copy(f32[4,8,512]{2,1,0:T(8,128)S(1)} %get-tuple-element.5) | data formatting | bytes 131072

commit v4 on v3

--- a/solution.py
+++ b/solution.py
@@ -133,57 +133,66 @@
     return mesh.shape["tracer"] == LINE and mesh.shape["band"] > 1
 
 
-def piece(c, rows):
+def last_parts(levels):
+    return 3 if levels % (3 * STRIP) == 0 else 1
+
+
+def piece(c, rows, levels):
     if isinstance(c, int) and c == 0:
-        return pl.ds(0, 4)
-    if isinstance(c, int) and c == rows - 1:
-        return pl.ds(3 * c + 1, 2)
-    return pl.ds(3 * c + 1, 3)
+        return pl.ds(0, 4), pl.ds(0, levels)
+    if isinstance(c, int) and c >= rows - 1:
+        depth = levels // last_parts(levels)
+        return pl.ds(3 * rows - 2, 2), pl.ds((c - rows + 1) * depth, depth)
+    return pl.ds(3 * c + 1, 3), pl.ds(0, levels)
 
 
 def mirror(z):
     return z + 1 - 2 * lax.rem(z, 2)
 
 
-def transport_row(weather, emission, source, target, row, target_row, north, south, zonal):
+def transport_row(weather, emission, source, target, row, target_row, north, south, zonal, strips=None):
     tracers, _, levels, lons = source.shape
     sublane = lax.broadcasted_iota(jnp.int32, (STRIP, lons), 0)
     first_sublane, last_sublane = sublane == 0, sublane == STRIP - 1
-    strips = levels // STRIP
+    count = levels // STRIP
+    begin, end = strips or (0, count)
 
     def one(k, carry):
         def field(at, strip):
             return source[k, at, strip * STRIP : (strip + 1) * STRIP, :]
 
-        q = field(row, 0)
+        def item(index, strip):
+            levels_here = slice(strip * STRIP, (strip + 1) * STRIP)
+            return jnp.concatenate([weather[j, index, levels_here, :] for j in range(LINE)], axis=1)
+
+        q = field(row, begin)
         q_raised = pltpu.roll(q, STRIP - 1, 0)
         below = jnp.zeros((STRIP, lons), jnp.float32)
-        for strip in range(strips):
-            levels_here = slice(strip * STRIP, (strip + 1) * STRIP)
-
-            def item(index):
-                return jnp.concatenate([weather[j, index, levels_here, :] for j in range(LINE)], axis=1)
-
-            u = item(zonal)
+        if begin > 0:
+            q_below = field(row, begin - 1)
+            q_up = jnp.where(last_sublane, q_raised, pltpu.roll(q_below, STRIP - 1, 0))
+            below = pltpu.roll(item(zonal + 1, begin - 1) * (q_below - q_up), 1, 0)
+        for strip in range(begin, end):
+            u = item(zonal, strip)
             flux = u * jnp.where(u > 0.0, q, pltpu.roll(q, lons - 1, 1))
             result = q - flux + pltpu.roll(flux, 1, 1)
-            m = item(north)
+            m = item(north, strip)
             result = result - m * jnp.where(m > 0.0, q, field(row + 1, strip))
-            m = item(south)
+            m = item(south, strip)
             result = result + m * jnp.where(m > 0.0, field(row - 1, strip), q)
-            if strip < strips - 1:
+            if strip < count - 1:
                 q_next = field(row, strip + 1)
                 q_next_raised = pltpu.roll(q_next, STRIP - 1, 0)
                 q_up = jnp.where(last_sublane, q_next_raised, q_raised)
             else:
                 q_next = q_next_raised = None
                 q_up = jnp.where(last_sublane, q, q_raised)
-            flux = item(zonal + 1) * (q - q_up)
+            flux = item(zonal + 1, strip) * (q - q_up)
             lowered = pltpu.roll(flux, 1, 0)
             result = result - flux + jnp.where(first_sublane, below, lowered)
             if strip == 0:
                 result = result + jnp.where(first_sublane, emission[k, pl.ds(row - 1, 1), :], 0.0)
-            target[k, target_row, levels_here, :] = result
+            target[k, target_row, strip * STRIP : (strip + 1) * STRIP, :] = result
             q, q_raised, below = q_next, q_next_raised, lowered
         return carry
 
@@ -226,6 +235,8 @@
     z, b = lax.axis_index("tracer"), lax.axis_index("band")
     tracers, rows, levels, lons = state.shape
     regions = region_sigma.shape[1]
+    parts, strips = last_parts(levels), levels // STRIP
+    pieces = rows - 1 + parts
     halo_item, closed_item = 3 * rows, 3 * rows + 1
     near, far = mirror(z), jnp.where(z < 2, 2, 1)
     beyond, beyond_next = 3 - z, mirror(3 - z)
@@ -239,14 +250,18 @@
         )
 
     barrier = pltpu.get_barrier_semaphore()
-    for step in range(1, LINE):
-        pl.semaphore_signal(
-            barrier, inc=1, device_id={"tracer": lax.rem(z + step, LINE)}, device_id_type=pl.DeviceIdType.MESH
-        )
+    def enter(**where):
+        pl.semaphore_signal(barrier, inc=1, device_id=where, device_id_type=pl.DeviceIdType.MESH)
+
+    enter(tracer=near)
+
+    @pl.when(inner)
+    def _():
+        enter(tracer=beyond)
+        enter(tracer=beyond_next)
+
     for step in range(1, bands):
-        pl.semaphore_signal(
-            barrier, inc=1, device_id={"band": lax.rem(b + step, bands)}, device_id_type=pl.DeviceIdType.MESH
-        )
+        enter(band=lax.rem(b + step, bands))
 
     def own_item(c, index, array, row):
         return pltpu.make_async_copy(array.at[row], weather.at[z, index], own_sem.at[c])
@@ -277,15 +292,16 @@
     for load in load_tables:
         load.start()
 
-    pl.semaphore_wait(barrier, LINE - 1 + bands - 1)
+    pl.semaphore_wait(barrier, 2 + bands - 1)
 
     def piece_copy(c, owner, target, sems, slot):
-        part = weather.at[owner, piece(c, rows)]
+        part = weather.at[owner, *piece(c, rows, levels)]
         return send(part, part, sems.at[c, slot], piece_recv.at[c, owner], tracer=target)
 
-    for c in range(rows):
-        part = weather.at[z, piece(c, rows)]
-        pltpu.make_async_copy(part, part, own_sem.at[c]).wait()
+    for c in range(pieces):
+        if c < rows:
+            part = weather.at[z, piece(c, rows, levels)[0]]
+            pltpu.make_async_copy(part, part, own_sem.at[c]).wait()
         piece_copy(c, z, near, piece_send, 0).start()
         piece_copy(c, z, far, piece_send, 1).start()
 
@@ -373,7 +389,7 @@
 
     def arrive(c):
         def wait_for(owner):
-            part = weather.at[owner, piece(c, rows)]
+            part = weather.at[owner, *piece(c, rows, levels)]
             pltpu.make_async_copy(part, part, piece_recv.at[c, owner]).wait()
 
         for slot, owner in enumerate((beyond, beyond_next)):
@@ -389,8 +405,8 @@
     one_step = functools.partial(transport_row, weather, emission, first, second)
     two_step = functools.partial(transport_row, weather, emission, second, final)
 
-    def second_step(row, north, south, zonal):
-        two_step(row + 1, row, north, south, zonal)
+    def second_step(row, north, south, zonal, part=None):
+        two_step(row + 1, row, north, south, zonal, part)
 
     arrive(0)
 
@@ -425,19 +441,22 @@
 
     lax.fori_loop(2, rows - 1, middle, 0)
 
-    c = rows - 1
-    arrive(c)
-    one_step(c, c, 0, 3 * c - 2, 3 * c + 1)
-    second_step(c - 2, 3 * c - 2, 3 * c - 5, 3 * c - 1)
-
     @pl.when(has_north)
     def _():
         pltpu.make_async_copy(second.at[:, rows + 1], second.at[:, rows + 1], edge_recv.at[3]).wait()
 
-    second_step(rows - 2, 0, 3 * c - 2, 3 * c + 1)
-    second_step(rows - 1, last_north, 0, 2)
-
-    for c in range(rows):
+    c, done = rows - 1, 0
+    for part in range(parts):
+        arrive(c + part)
+        here = (part * strips // parts, (part + 1) * strips // parts)
+        one_step(c, c, 0, 3 * c - 2, 3 * c + 1, here)
+        second_step(c - 2, 3 * c - 2, 3 * c - 5, 3 * c - 1, here)
+        second_step(c, last_north, 0, 2, here)
+        ready = here[1] if part == parts - 1 else here[1] - 1
+        second_step(c - 1, 0, 3 * c - 2, 3 * c + 1, (done, ready))
+        done = ready
+
+    for c in range(pieces):
         piece_copy(c, z, near, piece_send, 0).wait_send()
         piece_copy(c, z, far, piece_send, 1).wait_send()
 
@@ -473,6 +492,7 @@
 ):
     tracers, rows, levels, lons = tracer_state.shape
     bands = lax.axis_size("band")
+    pieces = rows - 1 + last_parts(levels)
     dma = pltpu.SemaphoreType.DMA
     vmem = pl.BlockSpec(memory_space=pltpu.VMEM)
     hbm = pl.BlockSpec(memory_space=pltpu.HBM)
@@ -510,9 +530,9 @@
             dma((4,)),
             dma((rows,)),
             dma((1,)),
-            dma((rows, 2)),
-            dma((rows, LINE)),
-            dma((rows, 2)),
+            dma((pieces, 2)),
+            dma((pieces, LINE)),
+            dma((pieces, 2)),
             dma((1,)),
             dma((bands,)),
             dma((bands,)),

time: 51.1 us -> 55 us (1.076)
  Pallas kernels: 48.1 us -> 51.9 us
    pallas_call x1, Pallas kernels: 48.1 us -> 51.9 us  [on_device_fused(): pl.pallas_call(functools.partial(window_kernel, bands), out_shape=(jax.Sh...]
where the time goes in v4:
time: 55 us; the launch traced here: 54.8 us
  Pallas kernels  51.9 us (94%)
  local copies, waits for them, and re-layouts  2.3 us (4%)
  between operations  0.64 us (1%)
    pallas_call x1, Pallas kernels, on_device_fused(): pl.pallas_call(functools.partial(window_kernel, bands), out_shape=(jax.Sh...  51.9 us
    unnamed x2, local copies, waits for them, and re-layouts  2.3 us

profile of v4, /device:TPU:0, one launch (start us, length us, event | category | flops | bytes accessed | tf_op | source)
XLA Modules:
  0.0 54.8 jit_solution(14709272081807864307)
XLA Ops:
  0.6 51.9 %shard_map.104 = (f32[4,8,48,512]{3,2,1,0:T(8,128)S(1)}, f32[4,8,512]{2,1,0:T(8,128)S(1)}) custom-call(s32[4,4]{1,0:T(4,128)} %tile_index_hbm.1, f32[4,22]{1,0:T(4,128)} %region_sigma_hbm.1, s32[8,512]{1,0:T(8,128)} %region_map_hbm.1, f32[8,8,8]{2,1,0:T(8,128)} %prior_tiles_hbm.1, f32[4,8,48,512]{3,2,1,0:T(8,128)} %state.1, f32[4,8,512]{2,1,0:T(8,128)} %control.1, ...), custom_call_target="tpu_custom_call" | custom-call | tf_op jit(solution)/shard_map/pallas_call | solution.py:513
  52.5 1.7 %copy.13 = f32[4,8,48,512]{3,2,1,0:T(8,128)} copy(f32[4,8,48,512]{3,2,1,0:T(8,128)S(1)} %get-tuple-element.4) | data formatting | bytes 6291456
  54.2 0.6 %copy.14 = f32[4,8,512]{2,1,0:T(8,128)} copy(f32[4,8,512]{2,1,0:T(8,128)S(1)} %get-tuple-element.5) | data formatting | bytes 131072

commit v5 on v4

--- a/solution.py
+++ b/solution.py
@@ -127,6 +127,7 @@
 
 LINE = 4
 STRIP = 8
+HOLD = 4
 
 
 def fits_fused(mesh):
@@ -157,7 +158,13 @@
     count = levels // STRIP
     begin, end = strips or (0, count)
 
-    def one(k, carry):
+    held_back = []
+
+    def store():
+        k, strip, result = held_back.pop(0)
+        target[k, target_row, strip * STRIP : (strip + 1) * STRIP, :] = result
+
+    def one(k):
         def field(at, strip):
             return source[k, at, strip * STRIP : (strip + 1) * STRIP, :]
 
@@ -192,11 +199,15 @@
             result = result - flux + jnp.where(first_sublane, below, lowered)
             if strip == 0:
                 result = result + jnp.where(first_sublane, emission[k, pl.ds(row - 1, 1), :], 0.0)
-            target[k, target_row, strip * STRIP : (strip + 1) * STRIP, :] = result
+            held_back.append((k, strip, result))
+            if len(held_back) > HOLD:
+                store()
             q, q_raised, below = q_next, q_next_raised, lowered
-        return carry
-
-    lax.fori_loop(0, tracers, one, 0)
+
+    for k in range(tracers):
+        one(k)
+    while held_back:
+        store()
 
 
 def window_kernel(

time: 55 us -> 52.9 us (0.962)
  Pallas kernels: 51.9 us -> 49.8 us
    pallas_call x1, Pallas kernels: 51.9 us -> 49.8 us  [on_device_fused(): pl.pallas_call(functools.partial(window_kernel, bands), out_shape=(jax.Sh...]
where the time goes in v5:
time: 52.9 us; the launch traced here: 52.8 us
  Pallas kernels  49.8 us (94%)
  local copies, waits for them, and re-layouts  2.3 us (4%)
  between operations  0.64 us (1%)
    pallas_call x1, Pallas kernels, on_device_fused(): pl.pallas_call(functools.partial(window_kernel, bands), out_shape=(jax.Sh...  49.8 us
    unnamed x2, local copies, waits for them, and re-layouts  2.3 us

profile of v5, /device:TPU:0, one launch (start us, length us, event | category | flops | bytes accessed | tf_op | source)
XLA Modules:
  0.0 52.8 jit_solution(10659642373526260339)
XLA Ops:
  0.6 49.8 %shard_map.104 = (f32[4,8,48,512]{3,2,1,0:T(8,128)S(1)}, f32[4,8,512]{2,1,0:T(8,128)S(1)}) custom-call(s32[4,4]{1,0:T(4,128)} %tile_index_hbm.1, f32[4,22]{1,0:T(4,128)} %region_sigma_hbm.1, s32[8,512]{1,0:T(8,128)} %region_map_hbm.1, f32[8,8,8]{2,1,0:T(8,128)} %prior_tiles_hbm.1, f32[4,8,48,512]{3,2,1,0:T(8,128)} %state.1, f32[4,8,512]{2,1,0:T(8,128)} %control.1, ...), custom_call_target="tpu_custom_call" | custom-call | tf_op jit(solution)/shard_map/pallas_call | solution.py:524
  50.5 1.7 %copy.13 = f32[4,8,48,512]{3,2,1,0:T(8,128)} copy(f32[4,8,48,512]{3,2,1,0:T(8,128)S(1)} %get-tuple-element.4) | data formatting | bytes 6291456
  52.1 0.6 %copy.14 = f32[4,8,512]{2,1,0:T(8,128)} copy(f32[4,8,512]{2,1,0:T(8,128)S(1)} %get-tuple-element.5) | data formatting | bytes 131072

commit v6 on v5

--- a/solution.py
+++ b/solution.py
@@ -128,6 +128,8 @@
 LINE = 4
 STRIP = 8
 HOLD = 4
+AHEAD = 2
+LAST_PARTS = 1
 
 
 def fits_fused(mesh):
@@ -135,7 +137,7 @@
 
 
 def last_parts(levels):
-    return 3 if levels % (3 * STRIP) == 0 else 1
+    return LAST_PARTS if levels % (LAST_PARTS * STRIP) == 0 else 1
 
 
 def piece(c, rows, levels):
@@ -309,12 +311,15 @@
         part = weather.at[owner, *piece(c, rows, levels)]
         return send(part, part, sems.at[c, slot], piece_recv.at[c, owner], tracer=target)
 
-    for c in range(pieces):
-        if c < rows:
-            part = weather.at[z, piece(c, rows, levels)[0]]
-            pltpu.make_async_copy(part, part, own_sem.at[c]).wait()
+    def feed(c):
         piece_copy(c, z, near, piece_send, 0).start()
         piece_copy(c, z, far, piece_send, 1).start()
+
+    for c in range(rows):
+        part = weather.at[z, piece(c, rows, levels)[0]]
+        pltpu.make_async_copy(part, part, own_sem.at[c]).wait()
+        if c < AHEAD:
+            feed(c)
 
     def edge_copy(slot):
         src, dst, step = (
@@ -399,6 +404,21 @@
         pltpu.make_async_copy(first.at[:, rows + 1], first.at[:, rows + 1], edge_recv.at[1]).wait()
 
     def arrive(c):
+        if isinstance(c, int):
+            if c + AHEAD < pieces:
+                feed(c + AHEAD)
+        else:
+
+            @pl.when(c + AHEAD < rows - 1)
+            def _():
+                feed(c + AHEAD)
+
+            for later in range(rows - 1, pieces):
+
+                @pl.when(c + AHEAD == later)
+                def _():
+                    feed(later)
+
         def wait_for(owner):
             part = weather.at[owner, *piece(c, rows, levels)]
             pltpu.make_async_copy(part, part, piece_recv.at[c, owner]).wait()

time: 52.9 us -> 58.9 us (1.11)
  the two profiles are of different devices: /device:TPU:0 before, /device:TPU:1 now
where the time goes in v6:
time: 58.9 us; the launch traced here: 58.8 us
  Pallas kernels  55.8 us (95%)
  local copies, waits for them, and re-layouts  2.3 us (4%)
  between operations  0.64 us (1%)
    pallas_call x1, Pallas kernels, on_device_fused(): pl.pallas_call(functools.partial(window_kernel, bands), out_shape=(jax.Sh...  55.8 us
    unnamed x2, local copies, waits for them, and re-layouts  2.3 us

profile of v6, /device:TPU:1, one launch (start us, length us, event | category | flops | bytes accessed | tf_op | source)
XLA Modules:
  0.0 58.8 jit_solution(533245380046011064)
XLA Ops:
  0.6 55.8 %shard_map.104 = (f32[4,8,48,512]{3,2,1,0:T(8,128)S(1)}, f32[4,8,512]{2,1,0:T(8,128)S(1)}) custom-call(s32[4,4]{1,0:T(4,128)} %tile_index_hbm.1, f32[4,22]{1,0:T(4,128)} %region_sigma_hbm.1, s32[8,512]{1,0:T(8,128)} %region_map_hbm.1, f32[8,8,8]{2,1,0:T(8,128)} %prior_tiles_hbm.1, f32[4,8,48,512]{3,2,1,0:T(8,128)} %state.1, f32[4,8,512]{2,1,0:T(8,128)} %control.1, ...), custom_call_target="tpu_custom_call" | custom-call | tf_op jit(solution)/shard_map/pallas_call | solution.py:544
  56.5 1.7 %copy.13 = f32[4,8,48,512]{3,2,1,0:T(8,128)} copy(f32[4,8,48,512]{3,2,1,0:T(8,128)S(1)} %get-tuple-element.4) | data formatting | bytes 6291456
  58.1 0.6 %copy.14 = f32[4,8,512]{2,1,0:T(8,128)} copy(f32[4,8,512]{2,1,0:T(8,128)S(1)} %get-tuple-element.5) | data formatting | bytes 131072

commit v7 on v5

--- a/solution.py
+++ b/solution.py
@@ -128,6 +128,7 @@
 LINE = 4
 STRIP = 8
 HOLD = 4
+LAST_PARTS = 1
 
 
 def fits_fused(mesh):
@@ -135,7 +136,7 @@
 
 
 def last_parts(levels):
-    return 3 if levels % (3 * STRIP) == 0 else 1
+    return LAST_PARTS if levels % (LAST_PARTS * STRIP) == 0 else 1
 
 
 def piece(c, rows, levels):
@@ -442,11 +443,15 @@
     @pl.when(has_south)
     def _():
         edge_copy(3).start()
-        pltpu.make_async_copy(second.at[:, 0], second.at[:, 0], edge_recv.at[2]).wait()
 
     def middle(c, carry):
         arrive(c)
         one_step(c, c, 3 * c + 1, 3 * c - 2, 3 * c + 2)
+
+        @pl.when(jnp.logical_and(has_south, c == 2))
+        def _():
+            pltpu.make_async_copy(second.at[:, 0], second.at[:, 0], edge_recv.at[2]).wait()
+
         second_step(c - 2, 3 * c - 2, jnp.where(c == 2, halo_item, 3 * c - 5), 3 * c - 1)
         return carry
 
@@ -488,6 +493,16 @@
     def _():
         for slot in (1, 3):
             edge_copy(slot).wait_send()
+
+
+def move_out(final, emission, final_out, emission_out, sems):
+    tracers = final.shape[0]
+    copies = [pltpu.make_async_copy(emission, emission_out, sems.at[tracers])]
+    copies += [pltpu.make_async_copy(final.at[k], final_out.at[k], sems.at[k]) for k in range(tracers)]
+    for copy in copies:
+        copy.start()
+    for copy in copies:
+        copy.wait()
 
 
 def on_device_fused(
@@ -521,12 +536,9 @@
             vertical_diffusion,
         )
     ]
-    return pl.pallas_call(
+    results = pl.pallas_call(
         functools.partial(window_kernel, bands),
-        out_shape=(
-            jax.ShapeDtypeStruct(tracer_state.shape, jnp.float32),
-            jax.ShapeDtypeStruct(control.shape, jnp.float32),
-        ),
+        out_shape=(pltpu.VMEM(tracer_state.shape, jnp.float32), pltpu.VMEM(control.shape, jnp.float32)),
         in_specs=[hbm] * len(operands),
         out_specs=(vmem, vmem),
         scratch_shapes=[
@@ -554,6 +566,17 @@
             collective_id=0, has_side_effects=True, vmem_limit_bytes=40 * 1024 * 1024
         ),
     )(*operands)
+    return pl.pallas_call(
+        move_out,
+        out_shape=(
+            jax.ShapeDtypeStruct(tracer_state.shape, jnp.float32),
+            jax.ShapeDtypeStruct(control.shape, jnp.float32),
+        ),
+        in_specs=[vmem, vmem],
+        out_specs=(hbm, hbm),
+        scratch_shapes=[dma((tracers + 1,))],
+        compiler_params=pltpu.CompilerParams(vmem_limit_bytes=8 * 1024 * 1024),
+    )(*[pltpu.with_memory_space_constraint(result, pltpu.VMEM) for result in results])
 
 
 def solution(mesh):

time: 52.9 us -> 53.2 us (level)
  Pallas kernels: 49.8 us -> 52.4 us
  local copies, waits for them, and re-layouts: 2.3 us -> 0 us
    pallas_call x1 -> x2, Pallas kernels: 49.8 us -> 52.4 us  [the longest x1 50.6 us: on_device_fused(): pl.pallas_call(functools.partial(window_kernel, bands), out_shape=(pltpu....]
    unnamed x2 -> x0, local copies, waits for them, and re-layouts: 2.3 us -> none
where the time goes in v7:
time: 53.2 us; the launch traced here: 53 us
  Pallas kernels  52.4 us (98%)
  between operations  0.64 us (1%)
    pallas_call x1, Pallas kernels, on_device_fused(): pl.pallas_call(functools.partial(window_kernel, bands), out_shape=(pltpu....  50.6 us
    pallas_call x1, Pallas kernels, on_device_fused(): pl.pallas_call(move_out, out_shape=(jax.ShapeDtypeStruct(tracer_state.sha...  1.72 us

profile of v7, /device:TPU:0, one launch (start us, length us, event | category | flops | bytes accessed | tf_op | source)
XLA Modules:
  0.0 53.0 jit_solution(17878716459847161166)
XLA Ops:
  0.6 50.6 %shard_map.104 = (f32[4,8,48,512]{3,2,1,0:T(8,128)S(1)}, f32[4,8,512]{2,1,0:T(8,128)S(1)}) custom-call(s32[4,4]{1,0:T(4,128)} %tile_index_hbm.1, f32[4,22]{1,0:T(4,128)} %region_sigma_hbm.1, s32[8,512]{1,0:T(8,128)} %region_map_hbm.1, f32[8,8,8]{2,1,0:T(8,128)} %prior_tiles_hbm.1, f32[4,8,48,512]{3,2,1,0:T(8,128)} %state.1, f32[4,8,512]{2,1,0:T(8,128)} %control.1, ...), custom_call_target="tpu_custom_call" | custom-call | tf_op jit(solution)/shard_map/pallas_call | solution.py:539
  51.3 1.7 %shard_map.105 = (f32[4,8,48,512]{3,2,1,0:T(8,128)}, f32[4,8,512]{2,1,0:T(8,128)}) custom-call(f32[4,8,48,512]{3,2,1,0:T(8,128)S(1)} %get-tuple-element.4.final, f32[4,8,512]{2,1,0:T(8,128)S(1)} %get-tuple-element.5.emission), custom_call_target="tpu_custom_call" | custom-call | tf_op jit(solution)/shard_map/pallas_call | solution.py:569

commit v8 on v7

--- a/solution.py
+++ b/solution.py
@@ -265,13 +265,8 @@
     def enter(**where):
         pl.semaphore_signal(barrier, inc=1, device_id=where, device_id_type=pl.DeviceIdType.MESH)
 
-    enter(tracer=near)
-
-    @pl.when(inner)
-    def _():
-        enter(tracer=beyond)
-        enter(tracer=beyond_next)
-
+    for step in range(1, LINE):
+        enter(tracer=lax.rem(z + step, LINE))
     for step in range(1, bands):
         enter(band=lax.rem(b + step, bands))
 
@@ -304,7 +299,7 @@
     for load in load_tables:
         load.start()
 
-    pl.semaphore_wait(barrier, 2 + bands - 1)
+    pl.semaphore_wait(barrier, LINE - 1 + bands - 1)
 
     def piece_copy(c, owner, target, sems, slot):
         part = weather.at[owner, *piece(c, rows, levels)]

time: 53.2 us -> 54.2 us (1.019)
  Pallas kernels: 52.4 us -> 53.4 us
    pallas_call x1, Pallas kernels: 50.6 us -> 51.6 us  [on_device_fused(): pl.pallas_call(functools.partial(window_kernel, bands), out_shape=(pltpu....]
where the time goes in v8:
time: 54.2 us; the launch traced here: 54 us
  Pallas kernels  53.4 us (99%)
  between operations  0.64 us (1%)
    pallas_call x1, Pallas kernels, on_device_fused(): pl.pallas_call(functools.partial(window_kernel, bands), out_shape=(pltpu....  51.6 us
    pallas_call x1, Pallas kernels, on_device_fused(): pl.pallas_call(move_out, out_shape=(jax.ShapeDtypeStruct(tracer_state.sha...  1.72 us

profile of v8, /device:TPU:0, one launch (start us, length us, event | category | flops | bytes accessed | tf_op | source)
XLA Modules:
  0.0 54.0 jit_solution(8762277398609518824)
XLA Ops:
  0.6 51.6 %shard_map.104 = (f32[4,8,48,512]{3,2,1,0:T(8,128)S(1)}, f32[4,8,512]{2,1,0:T(8,128)S(1)}) custom-call(s32[4,4]{1,0:T(4,128)} %tile_index_hbm.1, f32[4,22]{1,0:T(4,128)} %region_sigma_hbm.1, s32[8,512]{1,0:T(8,128)} %region_map_hbm.1, f32[8,8,8]{2,1,0:T(8,128)} %prior_tiles_hbm.1, f32[4,8,48,512]{3,2,1,0:T(8,128)} %state.1, f32[4,8,512]{2,1,0:T(8,128)} %control.1, ...), custom_call_target="tpu_custom_call" | custom-call | tf_op jit(solution)/shard_map/pallas_call | solution.py:534
  52.3 1.7 %shard_map.105 = (f32[4,8,48,512]{3,2,1,0:T(8,128)}, f32[4,8,512]{2,1,0:T(8,128)}) custom-call(f32[4,8,48,512]{3,2,1,0:T(8,128)S(1)} %get-tuple-element.4.final, f32[4,8,512]{2,1,0:T(8,128)S(1)} %get-tuple-element.5.emission), custom_call_target="tpu_custom_call" | custom-call | tf_op jit(solution)/shard_map/pallas_call | solution.py:564

commit v9 on v8

--- a/solution.py
+++ b/solution.py
@@ -127,7 +127,6 @@
 
 LINE = 4
 STRIP = 8
-HOLD = 4
 LAST_PARTS = 1
 
 
@@ -159,13 +158,7 @@
     count = levels // STRIP
     begin, end = strips or (0, count)
 
-    held_back = []
-
-    def store():
-        k, strip, result = held_back.pop(0)
-        target[k, target_row, strip * STRIP : (strip + 1) * STRIP, :] = result
-
-    def one(k):
+    def one(k, carry):
         def field(at, strip):
             return source[k, at, strip * STRIP : (strip + 1) * STRIP, :]
 
@@ -200,15 +193,11 @@
             result = result - flux + jnp.where(first_sublane, below, lowered)
             if strip == 0:
                 result = result + jnp.where(first_sublane, emission[k, pl.ds(row - 1, 1), :], 0.0)
-            held_back.append((k, strip, result))
-            if len(held_back) > HOLD:
-                store()
+            target[k, target_row, strip * STRIP : (strip + 1) * STRIP, :] = result
             q, q_raised, below = q_next, q_next_raised, lowered
-
-    for k in range(tracers):
-        one(k)
-    while held_back:
-        store()
+        return carry
+
+    lax.fori_loop(0, tracers, one, 0)
 
 
 def window_kernel(
@@ -412,60 +401,64 @@
     one_step = functools.partial(transport_row, weather, emission, first, second)
     two_step = functools.partial(transport_row, weather, emission, second, final)
 
-    def second_step(row, north, south, zonal, part=None):
-        two_step(row + 1, row, north, south, zonal, part)
-
-    arrive(0)
-
-    @pl.when(has_north)
-    def _():
-        edge_copy(4).start()
-
-    one_step(rows, rows, last_north, 0, 2)
-
-    @pl.when(has_north)
-    def _():
-        edge_copy(2).start()
-
-    arrive(1)
-
-    @pl.when(has_south)
-    def _():
-        pltpu.make_async_copy(weather.at[:, halo_item], weather.at[:, halo_item], edge_recv.at[4]).wait()
-
-    one_step(1, 1, 4, halo_item, 5)
-
-    @pl.when(has_south)
-    def _():
-        edge_copy(3).start()
-
-    def middle(c, carry):
-        arrive(c)
-        one_step(c, c, 3 * c + 1, 3 * c - 2, 3 * c + 2)
-
-        @pl.when(jnp.logical_and(has_south, c == 2))
+    def items(c):
+        ends = c == rows - 1
+        north = jnp.where(c == 0, last_north, jnp.where(ends, 0, 3 * c + 1))
+        south = jnp.where(c == 0, 0, jnp.where(c == 1, halo_item, 3 * c - 2))
+        return north, south, jnp.where(ends, 3 * c + 1, 3 * c + 2)
+
+    def wait_edge(slot, ref):
+        pltpu.make_async_copy(ref, ref, edge_recv.at[slot]).wait()
+
+    def turn(c, carry):
+        @pl.when(c < rows)
         def _():
-            pltpu.make_async_copy(second.at[:, 0], second.at[:, 0], edge_recv.at[2]).wait()
-
-        second_step(c - 2, 3 * c - 2, jnp.where(c == 2, halo_item, 3 * c - 5), 3 * c - 1)
+            @pl.when(c == 0)
+            def _():
+                arrive(0)
+
+            @pl.when(jnp.logical_and(c > 0, c < rows - 1))
+            def _():
+                arrive(c)
+
+            @pl.when(c == rows - 1)
+            def _():
+                arrive(rows - 1)
+
+            @pl.when(jnp.logical_and(has_north, c == 0))
+            def _():
+                edge_copy(4).start()
+
+            @pl.when(jnp.logical_and(has_south, c == 1))
+            def _():
+                wait_edge(4, weather.at[:, halo_item])
+
+            row = lax.rem(c + rows - 1, rows) + 1
+            one_step(row, row, *items(c))
+
+            @pl.when(jnp.logical_and(has_north, c == 0))
+            def _():
+                edge_copy(2).start()
+
+            @pl.when(jnp.logical_and(has_south, c == 1))
+            def _():
+                edge_copy(3).start()
+
+        @pl.when(c >= 2)
+        def _():
+            @pl.when(jnp.logical_and(has_south, c == 2))
+            def _():
+                wait_edge(2, second.at[:, 0])
+
+            @pl.when(jnp.logical_and(has_north, c == rows + 1))
+            def _():
+                wait_edge(3, second.at[:, rows + 1])
+
+            two_step(c - 1, c - 2, *items(lax.rem(c - 1, rows)))
+
         return carry
 
-    lax.fori_loop(2, rows - 1, middle, 0)
-
-    @pl.when(has_north)
-    def _():
-        pltpu.make_async_copy(second.at[:, rows + 1], second.at[:, rows + 1], edge_recv.at[3]).wait()
-
-    c, done = rows - 1, 0
-    for part in range(parts):
-        arrive(c + part)
-        here = (part * strips // parts, (part + 1) * strips // parts)
-        one_step(c, c, 0, 3 * c - 2, 3 * c + 1, here)
-        second_step(c - 2, 3 * c - 2, 3 * c - 5, 3 * c - 1, here)
-        second_step(c, last_north, 0, 2, here)
-        ready = here[1] if part == parts - 1 else here[1] - 1
-        second_step(c - 1, 0, 3 * c - 2, 3 * c + 1, (done, ready))
-        done = ready
+    lax.fori_loop(0, rows + 2, turn, 0)
 
     for c in range(pieces):
         piece_copy(c, z, near, piece_send, 0).wait_send()

time: 54.2 us -> 50.7 us (0.935)
  Pallas kernels: 53.4 us -> 50 us
    pallas_call x1, Pallas kernels: 51.6 us -> 48.2 us  [on_device_fused(): pl.pallas_call(functools.partial(window_kernel, bands), out_shape=(pltpu....]
where the time goes in v9:
time: 50.7 us; the launch traced here: 50.6 us
  Pallas kernels  50 us (99%)
  between operations  0.64 us (1%)
    pallas_call x1, Pallas kernels, on_device_fused(): pl.pallas_call(functools.partial(window_kernel, bands), out_shape=(pltpu....  48.2 us
    pallas_call x1, Pallas kernels, on_device_fused(): pl.pallas_call(move_out, out_shape=(jax.ShapeDtypeStruct(tracer_state.sha...  1.72 us

profile of v9, /device:TPU:0, one launch (start us, length us, event | category | flops | bytes accessed | tf_op | source)
XLA Modules:
  0.0 50.6 jit_solution(14741991194837586203)
XLA Ops:
  0.6 48.2 %shard_map.104 = (f32[4,8,48,512]{3,2,1,0:T(8,128)S(1)}, f32[4,8,512]{2,1,0:T(8,128)S(1)}) custom-call(s32[4,4]{1,0:T(4,128)} %tile_index_hbm.1, f32[4,22]{1,0:T(4,128)} %region_sigma_hbm.1, s32[8,512]{1,0:T(8,128)} %region_map_hbm.1, f32[8,8,8]{2,1,0:T(8,128)} %prior_tiles_hbm.1, f32[4,8,48,512]{3,2,1,0:T(8,128)} %state.1, f32[4,8,512]{2,1,0:T(8,128)} %control.1, ...), custom_call_target="tpu_custom_call" | custom-call | tf_op jit(solution)/shard_map/pallas_call | solution.py:527
  48.9 1.7 %shard_map.105 = (f32[4,8,48,512]{3,2,1,0:T(8,128)}, f32[4,8,512]{2,1,0:T(8,128)}) custom-call(f32[4,8,48,512]{3,2,1,0:T(8,128)S(1)} %get-tuple-element.4.final, f32[4,8,512]{2,1,0:T(8,128)S(1)} %get-tuple-element.5.emission), custom_call_target="tpu_custom_call" | custom-call | tf_op jit(solution)/shard_map/pallas_call | solution.py:557

commit v10 on v9

--- a/solution.py
+++ b/solution.py
@@ -254,8 +254,12 @@
     def enter(**where):
         pl.semaphore_signal(barrier, inc=1, device_id=where, device_id_type=pl.DeviceIdType.MESH)
 
-    for step in range(1, LINE):
-        enter(tracer=lax.rem(z + step, LINE))
+    enter(tracer=near)
+
+    @pl.when(inner)
+    def _():
+        enter(tracer=beyond)
+        enter(tracer=beyond_next)
     for step in range(1, bands):
         enter(band=lax.rem(b + step, bands))
 
@@ -288,7 +292,7 @@
     for load in load_tables:
         load.start()
 
-    pl.semaphore_wait(barrier, LINE - 1 + bands - 1)
+    pl.semaphore_wait(barrier, 2 + bands - 1)
 
     def piece_copy(c, owner, target, sems, slot):
         part = weather.at[owner, *piece(c, rows, levels)]

time: 50.7 us -> 49.8 us (0.982)
  Pallas kernels: 50 us -> 49 us
    pallas_call x1, Pallas kernels: 48.2 us -> 47.3 us  [on_device_fused(): pl.pallas_call(functools.partial(window_kernel, bands), out_shape=(pltpu....]
where the time goes in v10:
time: 49.8 us; the launch traced here: 49.7 us
  Pallas kernels  49 us (98%)
  between operations  0.64 us (1%)
    pallas_call x1, Pallas kernels, on_device_fused(): pl.pallas_call(functools.partial(window_kernel, bands), out_shape=(pltpu....  47.3 us
    pallas_call x1, Pallas kernels, on_device_fused(): pl.pallas_call(move_out, out_shape=(jax.ShapeDtypeStruct(tracer_state.sha...  1.72 us

profile of v10, /device:TPU:0, one launch (start us, length us, event | category | flops | bytes accessed | tf_op | source)
XLA Modules:
  0.0 49.7 jit_solution(2449046583340400247)
XLA Ops:
  0.6 47.3 %shard_map.104 = (f32[4,8,48,512]{3,2,1,0:T(8,128)S(1)}, f32[4,8,512]{2,1,0:T(8,128)S(1)}) custom-call(s32[4,4]{1,0:T(4,128)} %tile_index_hbm.1, f32[4,22]{1,0:T(4,128)} %region_sigma_hbm.1, s32[8,512]{1,0:T(8,128)} %region_map_hbm.1, f32[8,8,8]{2,1,0:T(8,128)} %prior_tiles_hbm.1, f32[4,8,48,512]{3,2,1,0:T(8,128)} %state.1, f32[4,8,512]{2,1,0:T(8,128)} %control.1, ...), custom_call_target="tpu_custom_call" | custom-call | tf_op jit(solution)/shard_map/pallas_call | solution.py:531
  47.9 1.7 %shard_map.105 = (f32[4,8,48,512]{3,2,1,0:T(8,128)}, f32[4,8,512]{2,1,0:T(8,128)}) custom-call(f32[4,8,48,512]{3,2,1,0:T(8,128)S(1)} %get-tuple-element.4.final, f32[4,8,512]{2,1,0:T(8,128)S(1)} %get-tuple-element.5.emission), custom_call_target="tpu_custom_call" | custom-call | tf_op jit(solution)/shard_map/pallas_call | solution.py:561
